TPU v7x, 256 devices: a whole 4x4x8 slice. The times are simulated.
256 devices in a mesh: row: 16 (over x_hi, z), col: 16 (over x_lo, y, core).
Axes of the slice: x: 4 (x_hi: 2, x_lo: 2; x = x_hi * 2 + x_lo), y: 4, z: 8, core: 2. Of those that a mesh axis runs over, the one named last changes fastest.
Arguments:
- inputs: bfloat16 [64, 1024, 2048], P(None, 'row', 'col'), may hold values from -6 to 6
- cotangent: bfloat16 [64, 1024, 2048], P(None, 'row', 'col'), may hold values from -6 to 6
- spectral_weight: bfloat16 [2, 128, 128, 4096], P(None, 'row', 'col'), may hold values from -12 to 12
- point_weight: bfloat16 [64, 64], replicated, may hold values from -0.75 to 0.75
- bias: float32 [64], replicated, may hold values from -3 to 3
Outputs:
- grad_input: bfloat16 [64, 1024, 2048], P(None, 'row', 'col')
- spectral_grad: float32 [2, 128, 128, 4096], P(None, 'row', 'col')
- pointwise_grad: float32 [64, 64], replicated
- bias_grad: float32 [64], replicated
All inputs are finite; a program needn't handle non-finite values.
Results may differ from a plain program's by a relative error of at most 0.015.
Values may be sent and summed in bfloat16 or wider, within the bound.
A program may use at most 128 MiB of HBM per device.

v0:
```python
import math

import jax
import jax.numpy as jnp
from jax import lax
from jax.sharding import PartitionSpec as P

K1 = 128
K2 = 128


def angles(first, second, total):
    phase = jnp.mod(first[:, None] * second[None, :], total).astype(jnp.float32) * (
        2.0 * math.pi / total
    )
    return (jnp.cos(phase).astype(jnp.bfloat16), jnp.sin(phase).astype(jnp.bfloat16))


def widen(table):
    return lax.optimization_barrier(table).astype(jnp.float32)


def normal_slope(value):
    cumul = 0.5 * (1.0 + jax.scipy.special.erf(value * (1.0 / math.sqrt(2.0))))
    dens = jnp.exp(-0.5 * value * value) * (1.0 / math.sqrt(2.0 * math.pi))
    return cumul + value * dens


def spectrum(field, scale):
    channels, rows, cols = field.shape
    n_row = lax.axis_size("row")
    n_col = lax.axis_size("col")
    total_y = rows * n_row
    total_x = cols * n_col
    highest = lax.Precision.HIGHEST
    local_x = lax.axis_index("col") * cols + jnp.arange(cols, dtype=jnp.int32)
    modes = jnp.arange(K2 // n_col * lax.axis_size("col"), dtype=jnp.int32)
    cos_x, sin_x = angles(local_x, modes, total_x)
    table = jnp.stack([cos_x, -sin_x], 1)
    partial_x = lax.psum_scatter(
        jnp.einsum("cyx,xpk->kpcy", field, table, preferred_element_type=jnp.float32),
        "col",
        scatter_dimension=0,
        tiled=True,
    )
    real_part = partial_x[:, 0]
    imag_part = partial_x[:, 1]
    local_y = lax.axis_index("row") * rows + jnp.arange(rows, dtype=jnp.int32)
    modes = jnp.arange(K1 // n_row * lax.axis_size("row"), dtype=jnp.int32) - K1 // 2
    cos_y, sin_y = angles(local_y, modes, total_y)
    cos_f = widen(cos_y)
    sin_f = widen(sin_y)
    out_r = jnp.einsum("kcy,yj->jkc", real_part, cos_f, precision=highest) + jnp.einsum(
        "kcy,yj->jkc", imag_part, sin_f, precision=highest
    )
    out_i = jnp.einsum("kcy,yj->jkc", imag_part, cos_f, precision=highest) - jnp.einsum(
        "kcy,yj->jkc", real_part, sin_f, precision=highest
    )
    return (
        lax.psum_scatter(jnp.stack([out_r, out_i], 1), "row", scatter_dimension=0, tiled=True)
        * scale
    )


def spatial(blocks, rows, cols, scale):
    n_row = lax.axis_size("row")
    n_col = lax.axis_size("col")
    total_y = rows * n_row
    total_x = cols * n_col
    k1_local = blocks.shape[0]
    k2_local = blocks.shape[2]
    channels = blocks.shape[3]
    local_y = lax.axis_index("row") * rows + jnp.arange(rows, dtype=jnp.int32)
    modes_y = jnp.arange(K1, dtype=jnp.int32) - K1 // 2
    cos_y, sin_y = angles(modes_y, local_y, total_y)
    gathered = lax.all_gather(blocks, ("row", "col"), axis=0, tiled=True)
    gathered = gathered.reshape(n_row, n_col, k1_local, 2, k2_local, channels)
    gathered = jnp.transpose(gathered, (0, 2, 3, 1, 4, 5)).reshape(
        n_row * k1_local, 2, n_col * k2_local, channels
    )
    spec_r = gathered[:, 0]
    spec_i = gathered[:, 1]
    local_x = lax.axis_index("col") * cols + jnp.arange(cols, dtype=jnp.int32)
    modes_x = jnp.arange(K2, dtype=jnp.int32)
    cos_x, sin_x = angles(modes_x, local_x, total_x)
    table_x = jnp.stack([cos_x, -sin_x], 0)
    part_r = jnp.einsum(
        "jkc,jy->cyk", spec_r, cos_y, preferred_element_type=jnp.float32
    ) - jnp.einsum("jkc,jy->cyk", spec_i, sin_y, preferred_element_type=jnp.float32)
    part_i = jnp.einsum(
        "jkc,jy->cyk", spec_r, sin_y, preferred_element_type=jnp.float32
    ) + jnp.einsum("jkc,jy->cyk", spec_i, cos_y, preferred_element_type=jnp.float32)
    middle = jnp.stack([part_r, part_i], 2).astype(jnp.bfloat16)
    return jnp.einsum("cypk,pkx->cyx", middle, table_x, preferred_element_type=jnp.float32) * scale


def body(inputs, cotangent, spectral_weight, point_weight, bias):
    channels, rows, cols = inputs.shape
    scale = float(rows * lax.axis_size("row") * cols * lax.axis_size("col")) ** (-0.5)
    highest = lax.Precision.HIGHEST
    k1_local = spectral_weight.shape[1]
    k2_local = spectral_weight.shape[2]
    weight = spectral_weight.astype(jnp.float32).reshape(2, k1_local, k2_local, channels, channels)
    u_hat = spectrum(inputs, scale)
    ur, ui = (u_hat[:, 0], u_hat[:, 1])
    s_r = jnp.einsum("jkc,jkco->jko", ur, weight[0], precision=highest) - jnp.einsum(
        "jkc,jkco->jko", ui, weight[1], precision=highest
    )
    s_i = jnp.einsum("jkc,jkco->jko", ur, weight[1], precision=highest) + jnp.einsum(
        "jkc,jkco->jko", ui, weight[0], precision=highest
    )
    s_hat = jnp.stack([s_r, s_i], 1).astype(jnp.bfloat16)
    pre_act = (
        spatial(s_hat, rows, cols, scale)
        + jnp.einsum("cyx,co->oyx", inputs, point_weight, preferred_element_type=jnp.float32)
        + bias[:, None, None]
    )
    slope16 = (cotangent.astype(jnp.float32) * normal_slope(pre_act)).astype(jnp.bfloat16)
    point_term = jnp.einsum("cyx,oyx->co", inputs, slope16, preferred_element_type=jnp.float32)
    bias_term = jnp.sum(slope16.astype(jnp.float32), axis=(1, 2))
    pointwise_grad, bias_grad = lax.psum((point_term, bias_term), ("row", "col"))
    g_hat = spectrum(slope16, scale)
    gr, gi = (g_hat[:, 0], g_hat[:, 1])
    grad_r = jnp.einsum("jko,jkc->jkco", gr, ur) + jnp.einsum("jko,jkc->jkco", gi, ui)
    grad_i = jnp.einsum("jko,jkc->jkco", gi, ur) - jnp.einsum("jko,jkc->jkco", gr, ui)
    spectral_grad = jnp.stack([grad_r, grad_i], 0).reshape(
        2, k1_local, k2_local, channels * channels
    )
    du_r = jnp.einsum("jkco,jko->jkc", weight[0], gr, precision=highest) + jnp.einsum(
        "jkco,jko->jkc", weight[1], gi, precision=highest
    )
    du_i = jnp.einsum("jkco,jko->jkc", weight[0], gi, precision=highest) - jnp.einsum(
        "jkco,jko->jkc", weight[1], gr, precision=highest
    )
    du_hat = jnp.stack([du_r, du_i], 1).astype(jnp.bfloat16)
    grad_input = spatial(du_hat, rows, cols, scale) + jnp.einsum(
        "oyx,co->cyx", slope16, point_weight, preferred_element_type=jnp.float32
    )
    return (
        grad_input.astype(jnp.bfloat16),
        spectral_grad,
        pointwise_grad * scale,
        bias_grad * scale,
    )


def solution(mesh):
    in_specs = (P(None, "row", "col"), P(None, "row", "col"), P(None, "row", "col", None), P(), P())
    out_specs = (P(None, "row", "col"), P(None, "row", "col", None), P(), P())
    return jax.shard_map(body, mesh=mesh, in_specs=in_specs, out_specs=out_specs, check_vma=False)
```

profile of v0, /device:TPU:1, one launch (start us, length us, event | category | flops | bytes accessed | tf_op | source)
XLA Modules:
  0.0 1527.7 jit_solution(7948674883600630704)
XLA Ops:
  8.4 2.7 convolution_bitcast_fusion.1
  11.1 9.2 copy.59
  20.6 77.0 %reduce-scatter.5.cloned.1.call-done = f32[8,2,64,64]{3,2,1,0:T(8,128)} async-done(((f32[128,2,64,64]{3,2,1,0:T(8,128)}), f32[8,2,64,64]{3,2,1,0:T(8,128)}) %reduce-scatter.5.cloned.1.call-update) | async-done | bytes 262160 | tf_op jit(solution)/shard_map/reduce_scatter | solution.py:40
  97.6 1.2 fusion.69
  98.8 1.2 fusion.70
  100.0 1.2 fusion.60
  101.2 1.3 fusion.59
  102.6 1.4 copy.62
  105.3 2.1 squeeze.53
  107.4 193.3 %reduce-scatter.7.cloned.1.call-done = f32[8,2,8,64]{3,2,1,0:T(8,128)} async-done(((f32[128,2,8,64]{3,2,1,0:T(8,128)}), f32[8,2,8,64]{3,2,1,0:T(8,128)}) %reduce-scatter.7.cloned.1.call-update) | async-done | bytes 32784 | tf_op jit(solution)/shard_map/reduce_scatter | solution.py:60
  302.5 2.2 fusion.158
  307.9 2.2 fusion.67
  310.2 418.9 %all-gather.3.cloned.1.call-done = bf16[2048,2,8,64]{3,2,1,0:T(8,128)(2,1)} async-done(((bf16[8,2,8,64]{3,2,1,0:T(8,128)(2,1)}), bf16[2048,2,8,64]{3,2,1,0:T(8,128)(2,1)}) %all-gather.3.cloned.1.call-update) | async-done | bytes 4194320 | tf_op jit(solution)/shard_map/all_gather | solution.py:76
  729.0 9.1 copy.63
  738.1 6.0 fusion.154
  744.1 4.8 copy.100
  749.0 1.9 fusion.27
  750.9 2.0 fusion.25
  752.8 4.8 copy.99
  757.7 2.4 fusion.45
  761.9 3.3 convert_reduce_fusion
  765.2 2.7 convolution_bitcast_fusion
  767.8 9.2 copy.69
  777.1 71.7 %reduce-scatter.9.cloned.1.call-done = f32[8,2,64,64]{3,2,1,0:T(8,128)} async-done(((f32[128,2,64,64]{3,2,1,0:T(8,128)}), f32[8,2,64,64]{3,2,1,0:T(8,128)}) %reduce-scatter.9.cloned.1.call-update) | async-done | bytes 262160 | tf_op jit(solution)/shard_map/reduce_scatter | solution.py:40
  850.0 1.2 fusion.72
  851.2 1.2 fusion.58
  852.4 1.2 fusion.57
  853.7 1.4 copy.72
  855.4 196.2 %reduce-scatter.11.cloned.1.call-done = f32[8,2,8,64]{3,2,1,0:T(8,128)} async-done(((f32[128,2,8,64]{3,2,1,0:T(8,128)}), f32[8,2,8,64]{3,2,1,0:T(8,128)}) %reduce-scatter.11.cloned.1.call-update) | async-done | bytes 32784 | tf_op jit(solution)/shard_map/reduce_scatter | solution.py:60
  1052.5 2.9 fusion.160
  1055.4 3.0 fusion.163
  1058.4 1.7 fusion.161
  1060.1 1.7 fusion.162
  1063.8 79.7 %all-reduce = (f32[64,64]{0,1:T(8,128)S(1)}, f32[64]{0:T(128)S(1)}) all-reduce(f32[64,64]{0,1:T(8,128)S(1)} %convolution_bitcast_fusion.2, f32[64]{0:T(128)S(1)} %get-tuple-element.36), channel_id=1, replica_groups=mesh['row'=16,'col'=16] {'row','col'}, use_global_device_ids=true, to_apply=%region_4.5 | all-reduce | flops 4160 | bytes 33280 | tf_op jit(solution)/shard_map/psum | solution.py:121
  1144.7 2.2 fusion.64
  1146.9 2.2 multiply_add_fusion
  1149.1 3.0 stack.111
  1152.1 1.6 stack.112
  1153.7 3.1 pad_maximum_fusion
  1156.8 327.7 %all-gather.5.cloned.1.call-done = bf16[2048,2,8,64]{3,2,1,0:T(8,128)(2,1)} async-done(((bf16[8,2,8,64]{3,2,1,0:T(8,128)(2,1)}), bf16[2048,2,8,64]{3,2,1,0:T(8,128)(2,1)}) %all-gather.5.cloned.1.call-update) | async-done | bytes 4194320 | tf_op jit(solution)/shard_map/all_gather | solution.py:76
  1484.5 9.0 copy.73
  1493.5 6.1 fusion.153
  1499.6 4.8 copy.104
  1504.4 2.0 fusion.17
  1506.4 2.0 fusion.15
  1508.4 4.8 copy.103
  1513.2 2.4 fusion.51
  1517.2 3.3 fusion.14
  (69 shorter events, 16.8 us)
Async XLA Ops:
  7.2 1.2 copy-start
  7.2 90.4 %reduce-scatter.5.cloned.1.call-start = ((), (), s32[]{:S(2)}) async-start(), calls=%async_computation.4 | async-start | bytes 8912896 | tf_op jit(solution)/shard_map/reduce_scatter | solution.py:40
  20.3 280.4 %reduce-scatter.7.cloned.1.call-start = ((), (), s32[]{:S(2)}) async-start(), calls=%async_computation.5 | async-start | bytes 1114112 | tf_op jit(solution)/shard_map/reduce_scatter | solution.py:60
  101.2 2.8 copy-start.9
  104.0 625.1 %all-gather.3.cloned.1.call-start = ((), (), s32[]{:S(2)}) async-start(), calls=%async_computation.6 | async-start | bytes 8421376 | tf_op jit(solution)/shard_map/all_gather | solution.py:76
  105.3 200.3 %copy-start.5 = (bf16[8,8,64,64]{3,2,1,0:T(8,128)(2,1)}, bf16[8,8,64,64]{3,2,1,0:T(8,128)(2,1)S(1)}, u32[]{:S(2)}) copy-start(bf16[8,8,64,64]{3,2,1,0:T(8,128)(2,1)S(1)} %squeeze.51) | copy-start | bytes 1572868
  107.3 197.3 %copy-start.7 = (bf16[8,8,64,64]{3,2,1,0:T(8,128)(2,1)S(1)}, bf16[8,8,64,64]{3,2,1,0:T(8,128)(2,1)}, u32[]{:S(2)}) copy-start(bf16[8,8,64,64]{3,2,1,0:T(8,128)(2,1)} %squeeze.53) | copy-start | bytes 1572868
  302.5 5.5 copy-start.10
  307.2 541.6 %reduce-scatter.9.cloned.1.call-start = ((), (), s32[]{:S(2)}) async-start(), calls=%async_computation.7 | async-start | bytes 8912896 | tf_op jit(solution)/shard_map/reduce_scatter | solution.py:40
  757.6 2.4 copy-start.2
  760.0 1.6 copy-start.4
  760.0 1.8 copy-start.11
  760.1 1.8 copy-start.12
  777.0 274.5 %reduce-scatter.11.cloned.1.call-start = ((), (), s32[]{:S(2)}) async-start(), calls=%async_computation.8 | async-start | bytes 1114112 | tf_op jit(solution)/shard_map/reduce_scatter | solution.py:60
  855.1 205.1 %copy-start.6 = (bf16[8,8,64,64]{3,2,1,0:T(8,128)(2,1)S(1)}, bf16[8,8,64,64]{3,2,1,0:T(8,128)(2,1)}, u32[]{:S(2)}) copy-start(bf16[8,8,64,64]{3,2,1,0:T(8,128)(2,1)} %copy-done.5) | copy-start | bytes 1572868
  855.1 629.4 %all-gather.5.cloned.1.call-start = ((), (), s32[]{:S(2)}) async-start(), calls=%async_computation.9 | async-start | bytes 8421376 | tf_op jit(solution)/shard_map/all_gather | solution.py:76
  1051.6 6.9 copy-start.8
  1513.2 2.4 copy-start.1
  1515.6 1.6 copy-start.3
Sparse Core Ops, SparseCore 0:
  20.4 77.1 reduce-scatter.4
  104.1 196.5 reduce-scatter.6
  307.3 421.6 all-gather.2
  777.2 71.5 reduce-scatter.8
  855.2 196.3 reduce-scatter.10
  1062.7 421.7 all-gather.4
where the time goes:
time: 1540 us; the launch traced here: 1530 us
  waiting for transfers between devices  1280 us (83%)
  local copies, waits for them, and re-layouts  81.9 us (5%)
  blocking collectives  79.7 us (5%)
  matrix products  55.3 us (4%)
    all_gather x2, waiting for transfers between devices, spatial(): gathered = lax.all_gather(blocks, ('row', 'col'), axis=0, tiled=True)  747 us
    reduce_scatter x2, waiting for transfers between devices, spectrum(): lax.psum_scatter(jnp.stack([out_r, out_i], 1), 'row', scatter_dimension=0...  390 us
    reduce_scatter x2, waiting for transfers between devices, spectrum(): lax.psum_scatter(jnp.einsum('cyx,xpk->kpcy', field, table, preferred_elem...  149 us
    psum x1, blocking collectives, body(): lax.psum((point_term, bias_term), ('row', 'col'))  79.7 us
  transfers between devices with their start and end apart: 6, of which 6 were waited for; matrix products, arithmetic and copies ran while one was open for 1% of the time, Pallas kernels for 0%

commit v1 on v0

v1 whole, which is shorter than its diff:
```python
import functools
import math

import jax
import jax.numpy as jnp
import ml_dtypes
import numpy as np
from jax import lax
from jax.experimental import pallas as pl
from jax.experimental.pallas import tpu as pltpu
from jax.sharding import PartitionSpec as P

C = 64
K1 = 128
K2 = 128
NY = 1024
NX = 2048
TY = 64
TX = 128
N = 16
SCALE = float(NY * NX) ** (-0.5)
MESH = pl.DeviceIdType.MESH
BF = jnp.bfloat16
F32 = jnp.float32

X1, Y1, T1, T2, Y2, X2, X3, Y3, T3, T4, Y4, X4, Z1, Z2, Z3 = range(15)


def trig(first, second, total):
    phase = np.mod(first[:, None] * second[None, :], total).astype(np.float32) * np.float32(
        2.0 * math.pi / total
    )
    return np.cos(phase).astype(ml_dtypes.bfloat16), np.sin(phase).astype(ml_dtypes.bfloat16)


@functools.cache
def tables():
    cos, sin = trig(np.arange(K2), np.arange(NX), NX)
    tx = np.stack([cos.reshape(N, 8, NX), -sin.reshape(N, 8, NX)], 1).reshape(2 * K2, 4, NX // 4)
    tx = np.ascontiguousarray(tx.transpose(1, 0, 2))
    cos, sin = trig(np.arange(K1) - K1 // 2, np.arange(NY), NY)
    ty = np.stack([cos.reshape(K1, N, TY), sin.reshape(K1, N, TY)], 2).reshape(K1, 2 * NY)
    tyi = np.concatenate([cos, sin], 0)
    c, m, _ = np.meshgrid(np.arange(4), np.arange(N), np.arange(8), indexing="ij")
    e1 = ((4 * m + c).reshape(-1, 1) == np.arange(C)).astype(ml_dtypes.bfloat16)
    e = (np.arange(C)[:, None] == np.arange(C * C)[None, :] // C).astype(ml_dtypes.bfloat16)
    sel = (np.arange(C * 16)[:, None] // 16 == np.arange(C)[None, :]).astype(ml_dtypes.bfloat16)
    return tx, ty, tyi, e1, e, sel


def dot(a, b):
    return lax.dot_general(a, b, (((1,), (0,)), ((), ())), preferred_element_type=F32)


def dot_t(a, b):
    return lax.dot_general(a, b, (((1,), (1,)), ((), ())), preferred_element_type=F32)


def normal_slope(value):
    cumul = 0.5 * (1.0 + lax.erf(value * (1.0 / math.sqrt(2.0))))
    dens = jnp.exp(-0.5 * value * value) * (1.0 / math.sqrt(2.0 * math.pi))
    return cumul + value * dens


def kernel(
    inp, cot, w, pw, bias, tx, ty, tyi, e1, e, sel,
    gin, sg, pg, bg,
    inp_v, cot_v, w_v, tx_v, ty_v, tyi_v, e1_v, e_v, sel_v,
    xr, yr, tr, xsend, ysend, tsend,
    zsend, zr, f2_v, dz_v, dz2_v, kron_v, zp_v, gz_v, s_v, ue_v, sg_v, gin_v,
    send_sem, recv_sem, loc_sem,
):
    row = lax.axis_index("row")
    col = lax.axis_index("col")
    diag = row == col
    lane_lo = lax.broadcasted_iota(jnp.int32, (16, 128), 1) < 64
    mask_j = (lax.broadcasted_iota(jnp.int32, (8, 8, 128), 2) & 7) == lax.broadcasted_iota(
        jnp.int32, (8, 8, 128), 0
    )

    def wrap(i):
        return lax.rem(i, N)

    def remote(src, dst, phase, to, slot, device):
        return pltpu.make_async_remote_copy(
            src_ref=src,
            dst_ref=dst,
            send_sem=send_sem.at[phase, to],
            recv_sem=recv_sem.at[phase, slot],
            device_id=device,
            device_id_type=MESH,
        )

    def wait_recv(dst, phase, slot):
        remote(dst, dst, phase, slot, slot, (row, col)).wait_recv()

    def send_row(src_of, dst, phase):
        @pl.loop(1, N)
        def _(d):
            r = wrap(row + d)
            remote(src_of(r), dst.at[row], phase, r, row, (r, col)).start()

    def send_col(src_of, dst, phase):
        @pl.loop(1, N)
        def _(d):
            m = wrap(col + d)
            remote(src_of(m), dst.at[col], phase, m, col, (row, m)).start()

    def wait_all(dst, phase, own):
        @pl.loop(1, N)
        def _(d):
            slot = wrap(own + d)
            wait_recv(dst.at[slot], phase, slot)

    def send_t(src, dst, phase, to_modes):
        @pl.loop(0, N)
        def _(i):
            @pl.when(jnp.logical_not(jnp.logical_and(diag, i == row)))
            def _():
                if to_modes:
                    remote(src.at[i], dst.at[col], phase, i, col, (i, row)).start()
                else:
                    remote(src.at[i], dst.at[row], phase, i, row, (col, i)).start()

        @pl.when(diag)
        def _():
            dst[row] = src[row]

    def wait_t(dst, phase):
        @pl.loop(0, N)
        def _(i):
            @pl.when(jnp.logical_not(jnp.logical_and(diag, i == row)))
            def _():
                wait_recv(dst.at[i], phase, i)

    barrier = pltpu.get_barrier_semaphore()

    @pl.loop(1, N)
    def _(d):
        pl.semaphore_signal(barrier, inc=1, device_id=(row, wrap(col + d)), device_id_type=MESH)
        pl.semaphore_signal(barrier, inc=1, device_id=(wrap(row + d), col), device_id_type=MESH)

    @pl.loop(0, N)
    def _(i):
        @pl.when(jnp.logical_not(jnp.logical_and(diag, i == row)))
        def _():
            pl.semaphore_signal(barrier, inc=1, device_id=(col, i), device_id_type=MESH)
            pl.semaphore_signal(barrier, inc=1, device_id=(i, row), device_id_type=MESH)

    loads = [
        pltpu.make_async_copy(src, dst, loc_sem.at[i])
        for i, (src, dst) in enumerate(
            [
                (sel, sel_v),
                (inp, inp_v),
                (tx, tx_v),
                (ty, ty_v),
                (w, w_v),
                (e1, e1_v),
                (e, e_v),
                (tyi, tyi_v),
                (cot, cot_v),
                (inp.at[pl.ds(4 * col, 4)], xr.at[0, col]),
            ]
        )
    ]
    for load in loads:
        load.start()
    pl.semaphore_wait(barrier, jnp.where(diag, 4 * N - 4, 4 * N - 2))

    send_col(lambda m: inp.at[pl.ds(4 * m, 4)], xr.at[0], X1)

    def pack(src, dst):
        for b in range(4):
            dst[:, 128 * b : 128 * b + 128] = src[:, 16 * b : 16 * b + 16, :].reshape(1024, 128)

    def build_kron(which):
        @pl.loop(0, 4)
        def _(i):
            rows = pl.ds(pl.multiple_of(256 * i, 256), 256)
            part = (dot_t if which == 0 else dot)(sel_v[rows, :], pw[...]).astype(BF)
            for j in range(4):
                full = dot_t(part, sel_v[256 * j : 256 * j + 256, :])
                same = (lax.broadcasted_iota(jnp.int32, (256, 256), 0) & 15) == (
                    lax.broadcasted_iota(jnp.int32, (256, 256), 1) & 15
                )
                kron_v[which, rows, 256 * j : 256 * j + 256] = jnp.where(same, full, 0.0).astype(BF)

    def apply_kron(which, src, dst):
        @pl.loop(0, 4)
        def _(i):
            rows = pl.ds(pl.multiple_of(256 * i, 256), 256)
            out = pl.ds(pl.multiple_of(16 * i, 16), 16)
            for h in range(2):
                res = dot(kron_v[which, rows, :], src[:, 256 * h : 256 * h + 256])
                for t in range(2):
                    y = 32 * h + 16 * t
                    dst[out, y : y + 16, :] = res[:, 128 * t : 128 * t + 128].reshape(16, 16, 128)

    def forward_x(src, phase, dst):
        acc = jnp.zeros((256, 256), F32)
        for i in range(4):
            g = lax.rem(lax.div(col, 4) + i, 4)
            blocks = []
            for t in range(4):
                slot = 4 * g + t

                @pl.when(slot != col)
                def _(slot=slot):
                    wait_recv(src.at[slot], phase, slot)

                blocks.append(src[slot].reshape(256, 128))
            acc = acc + dot_t(tx_v[g], jnp.concatenate(blocks, 1))
        dst[...] = acc.astype(BF).reshape(N, 16, 256)

    def forward_y(src, dst):
        acc = jnp.zeros((K1, 64), F32)
        for q in range(4):
            parts = []
            for t in range(4):
                b = src[4 * q + t].astype(F32)
                jb = jnp.concatenate([b[8:16], -b[0:8]], 0)
                rows = []
                for h in range(2):
                    bh = b[:, 128 * h : 128 * h + 128]
                    jh = jb[:, 128 * h : 128 * h + 128]
                    rows.append(jnp.where(lane_lo, bh, pltpu.roll(jh, 64, 1)))
                    rows.append(jnp.where(lane_lo, pltpu.roll(bh, 64, 1), jh))
                parts.append(jnp.concatenate(rows, 0).astype(BF))
            acc = acc + dot_t(ty_v[:, 512 * q : 512 * q + 512], jnp.concatenate(parts, 1))
        res = (acc * SCALE).astype(BF).astype(F32)
        dst[:, :, 0:64] = res.reshape(N, 8, 64)

    def to_modes(src):
        xt = src[...].reshape(128, 128).T
        rows = []
        for ri in range(2):
            cols = []
            for c in range(4):
                at = (2 * c + ri) * 8
                tile = xt[at : at + 8]
                cols.append(jnp.where(mask_j, tile[None], 0.0).reshape(64, 128))
            rows.append(jnp.concatenate(cols, 1))
        return dot(jnp.concatenate(rows, 0).astype(BF), e1_v[...])

    def from_modes(spec, dst):
        full = dot_t(spec.astype(BF), e1_v[...])
        tiles = []
        for c in range(4):
            for ri in range(2):
                part = full[64 * ri : 64 * ri + 64, 128 * c : 128 * c + 128].reshape(8, 8, 128)
                tiles.append(jnp.sum(jnp.where(mask_j, part, 0.0), axis=0))
        xt = jnp.concatenate(tiles + [jnp.zeros((64, 128), F32)], 0)
        dst[...] = xt.T.reshape(N, 8, 128)

    def inverse_y(src, dst):
        ht = src[...].reshape(128, 128).T
        first, second = [], []
        for c in range(4):
            hr, hi = ht[16 * c : 16 * c + 8], ht[16 * c + 8 : 16 * c + 16]
            first += [hr, hi]
            second += [-hi, hr]
        h = jnp.concatenate([jnp.concatenate(first, 0), jnp.concatenate(second, 0)], 1).astype(BF)
        d = dot(h, tyi_v[...])
        for a in range(8):
            for p in range(2):
                t0 = d[32 * p : 32 * p + 16, 128 * a : 128 * a + 128]
                t1 = d[32 * p + 16 : 32 * p + 32, 128 * a : 128 * a + 128]
                at = slice(128 * p, 128 * p + 128)
                dst[2 * a, :, at] = jnp.where(lane_lo, t0, pltpu.roll(t1, 64, 1)).astype(BF)
                dst[2 * a + 1, :, at] = jnp.where(lane_lo, pltpu.roll(t0, 64, 1), t1).astype(BF)

    def inverse_x(src, out, dst, phase):
        yt = src[...].reshape(256, 256).astype(F32).T.astype(BF)
        for i in range(4):
            g = lax.rem(lax.div(col, 4) + 1 + i, 4)
            res = (dot(yt, tx_v[g]) * SCALE).astype(BF)
            for t in range(4):
                m = 4 * g + t
                out[m] = res[:, 128 * t : 128 * t + 128].reshape(4, TY, TX)

                @pl.when(m != col)
                def _(m=m):
                    remote(out.at[m], dst.at[col], phase, m, col, (row, m)).start()

                @pl.when(m == col)
                def _(m=m):
                    dst[m] = out[m]

    tsend[...] = jnp.zeros_like(tsend)
    zsend[...] = jnp.zeros_like(zsend)
    loads[0].wait()
    build_kron(0)
    build_kron(1)
    loads[1].wait()
    pack(inp_v, f2_v)
    apply_kron(0, f2_v, zp_v)
    loads[2].wait()
    loads[9].wait()
    forward_x(xr.at[0], X1, ysend.at[0])
    send_row(lambda r: ysend.at[0, r], yr.at[0], Y1)
    yr[0, row] = ysend[0, row]
    loads[3].wait()
    wait_all(yr.at[0], Y1, row)
    forward_y(yr.at[0], tsend.at[0])
    send_t(tsend.at[0], tr.at[0], T1, True)
    loads[4].wait()
    loads[5].wait()
    loads[6].wait()
    wait_t(tr.at[0], T1)

    u = to_modes(tr.at[0]).astype(BF)

    def fold(t):
        return t[:, 0:128] + t[:, 128:256] + t[:, 256:384] + t[:, 384:512]

    def mix(i, carry):
        sr, si = carry
        at = pl.ds(pl.multiple_of(i * 512, 512), 512)
        ue = dot(u, e_v[:, at])
        ue_v[:, at] = ue
        ur, ui = ue[0:64], ue[64:128]
        wr = w_v[0, :, :, at].astype(F32).reshape(64, 512)
        wi = w_v[1, :, :, at].astype(F32).reshape(64, 512)
        return sr + fold(wr * ur - wi * ui), si + fold(wr * ui + wi * ur)

    zero = jnp.zeros((64, 128), F32)
    sr, si = lax.fori_loop(0, 8, mix, (zero, zero))
    both = jnp.concatenate([sr, si], 0)
    both = both + pltpu.roll(both, 64, 1)
    from_modes(both[:, 0:64], tsend.at[1])
    send_t(tsend.at[1], tr.at[1], T2, False)

    loads[7].wait()
    wait_t(tr.at[1], T2)
    inverse_y(tr.at[1], ysend.at[1])
    send_row(lambda r: ysend.at[1, r], yr.at[1], Y2)
    yr[1, row] = ysend[1, row]
    wait_all(yr.at[1], Y2, row)
    inverse_x(yr.at[1], xsend.at[0], xr.at[1], X2)

    loads[8].wait()

    @pl.loop(0, N)
    def _(i):
        m = wrap(col + i)

        @pl.when(i != 0)
        def _():
            wait_recv(xr.at[1, m], X2, m)

        at = pl.ds(4 * m, 4)
        for c in range(4):
            z = xr[1, m, c].astype(F32) + zp_v[4 * m + c] + bias[4 * m + c]
            dz = cot_v[4 * m + c].astype(F32) * normal_slope(z)
            dz_v[4 * m + c] = dz.astype(BF)

        @pl.when(i != 0)
        def _():
            remote(dz_v.at[at], xr.at[2, col], X3, m, col, (row, m)).start()

        @pl.when(i == 0)
        def _():
            xr[2, m] = dz_v[at]

    pack(dz_v, dz2_v)

    @pl.loop(0, 4)
    def _(o):
        cols = pl.ds(pl.multiple_of(256 * o, 256), 256)
        dzo = dz2_v[cols, :]
        same = (lax.broadcasted_iota(jnp.int32, (256, 256), 0) & 15) == (
            lax.broadcasted_iota(jnp.int32, (256, 256), 1) & 15
        )
        for i in range(4):
            prod = dot_t(f2_v[256 * i : 256 * i + 256, :], dzo)
            prod = jnp.where(same, prod, 0.0).reshape(16, 16, 256)
            s_v[16 * i : 16 * i + 16, cols] = jnp.sum(prod, axis=1)
        s_v[64:72, cols] = dot_t(jnp.ones((16, 512), BF), dzo)[0:8]

    terms = s_v[...]
    high = terms.astype(BF)
    low = (terms - high.astype(F32)).astype(BF)
    terms = dot(high, sel_v[...]) + dot(low, sel_v[...])
    zsend[:, 0:4, 0:64] = terms[0:64].reshape(N, 4, 64)
    zsend[0, 4:5, 0:64] = terms[64:65]
    send_col(lambda m: zsend.at[m], zr.at[0], Z1)
    zr[0, col] = zsend[col]
    apply_kron(1, dz2_v, gz_v)

    forward_x(xr.at[2], X3, ysend.at[2])
    send_row(lambda r: ysend.at[2, r], yr.at[2], Y3)
    yr[2, row] = ysend[2, row]
    wait_all(zr.at[0], Z1, col)
    zr[3, 0] = jnp.sum(zr[0], axis=0)
    send_row(lambda r: zr.at[3, 0], zr.at[1], Z2)
    zr[1, row] = zr[3, 0]
    wait_all(yr.at[2], Y3, row)
    forward_y(yr.at[2], tsend.at[2])
    send_t(tsend.at[2], tr.at[2], T3, True)
    wait_all(zr.at[1], Z2, row)
    zr[3, 1] = jnp.sum(zr[1], axis=0)
    send_col(lambda m: zr.at[3, 1], zr.at[2], Z3)
    zr[2, col] = zr[3, 1]
    wait_t(tr.at[2], T3)

    g = to_modes(tr.at[2])
    g = jnp.concatenate([g, g], 1)
    gr, gi = g[0:64], g[64:128]
    gr4, gi4 = jnp.concatenate([gr] * 4, 1), jnp.concatenate([gi] * 4, 1)

    def mix_back(i, acc):
        at = pl.ds(pl.multiple_of(i * 512, 512), 512)
        wr = w_v[0, :, :, at].astype(F32).reshape(64, 512)
        wi = w_v[1, :, :, at].astype(F32).reshape(64, 512)
        both = jnp.concatenate([wr * gr4 + wi * gi4, wr * gi4 - wi * gr4], 0).astype(BF)
        return acc + dot_t(both, e_v[:, at])

    du = lax.fori_loop(0, 8, mix_back, jnp.zeros((128, 64), F32))
    from_modes(du, tsend.at[3])
    send_t(tsend.at[3], tr.at[3], T4, False)

    @pl.loop(0, 8)
    def _(i):
        at = pl.ds(pl.multiple_of(i * 512, 512), 512)
        ur, ui = ue_v[0:64, at], ue_v[64:128, at]
        sg_v[0, :, :, at] = (gr4 * ur + gi4 * ui).reshape(8, 8, 512)
        sg_v[1, :, :, at] = (gi4 * ur - gr4 * ui).reshape(8, 8, 512)

    out_sg = pltpu.make_async_copy(sg_v, sg, loc_sem.at[0])
    out_sg.start()

    wait_t(tr.at[3], T4)
    inverse_y(tr.at[3], ysend.at[3])
    send_row(lambda r: ysend.at[3, r], yr.at[3], Y4)
    yr[3, row] = ysend[3, row]
    wait_all(zr.at[2], Z3, col)
    pg[...] = zr[2, :, 0:4, 0:64].reshape(64, 64) * SCALE
    bg[...] = zr[2, 0, 4:5, 0:64] * SCALE
    wait_all(yr.at[3], Y4, row)
    inverse_x(yr.at[3], xsend.at[1], xr.at[3], X4)

    @pl.loop(0, N)
    def _(i):
        m = wrap(col + i)

        @pl.when(i != 0)
        def _():
            wait_recv(xr.at[3, m], X4, m)

        at = pl.ds(4 * m, 4)
        gin_v[at] = (xr[3, m].astype(F32) + gz_v[at]).astype(BF)

    out_gin = pltpu.make_async_copy(gin_v, gin, loc_sem.at[1])
    out_gin.start()

    def wait_send(src, phase, to):
        remote(src, src, phase, to, to, (row, col)).wait_send()

    @pl.loop(1, N)
    def _(d):
        m = wrap(col + d)
        r = wrap(row + d)
        wait_send(inp.at[pl.ds(4 * m, 4)], X1, m)
        wait_send(xsend.at[0, m], X2, m)
        wait_send(dz_v.at[pl.ds(4 * m, 4)], X3, m)
        wait_send(xsend.at[1, m], X4, m)
        wait_send(zsend.at[m], Z1, m)
        wait_send(zr.at[3, 1], Z3, m)
        wait_send(zr.at[3, 0], Z2, r)
        for i, phase in enumerate((Y1, Y2, Y3, Y4)):
            wait_send(ysend.at[i, r], phase, r)

    @pl.loop(0, N)
    def _(i):
        @pl.when(jnp.logical_not(jnp.logical_and(diag, i == row)))
        def _():
            for k, phase in enumerate((T1, T2, T3, T4)):
                wait_send(tsend.at[k, i], phase, i)

    out_sg.wait()
    out_gin.wait()


def body(inputs, cotangent, spectral_weight, point_weight, bias):
    any_spec = pl.BlockSpec(memory_space=pl.ANY)
    vmem = pl.BlockSpec(memory_space=pltpu.VMEM)
    smem = pl.BlockSpec(memory_space=pltpu.SMEM)
    consts = [jnp.asarray(t) for t in tables()]
    field = (C, TY, TX)
    grad_input, spectral_grad, pointwise_grad, bias_grad = pl.pallas_call(
        kernel,
        out_shape=(
            jax.ShapeDtypeStruct(field, BF),
            jax.ShapeDtypeStruct((2, 8, 8, C * C), F32),
            jax.ShapeDtypeStruct((C, C), F32),
            jax.ShapeDtypeStruct((1, C), F32),
        ),
        in_specs=[any_spec, any_spec, any_spec, vmem, smem] + [any_spec] * 6,
        out_specs=(any_spec, any_spec, vmem, vmem),
        scratch_shapes=[
            pltpu.VMEM(field, BF),
            pltpu.VMEM(field, BF),
            pltpu.VMEM((2, 8, 8, C * C), BF),
            *[pltpu.VMEM(t.shape, BF) for t in consts],
            pltpu.VMEM((4, N, 4, TY, TX), BF),
            pltpu.VMEM((4, N, 16, 256), BF),
            pltpu.VMEM((4, N, 8, 128), F32),
            pltpu.VMEM((2, N, 4, TY, TX), BF),
            pltpu.VMEM((4, N, 16, 256), BF),
            pltpu.VMEM((4, N, 8, 128), F32),
            pltpu.VMEM((N, 8, 128), F32),
            pltpu.VMEM((4, N, 8, 128), F32),
            pltpu.VMEM((1024, 512), BF),
            pltpu.VMEM(field, BF),
            pltpu.VMEM((1024, 512), BF),
            pltpu.VMEM((2, 1024, 1024), BF),
            pltpu.VMEM(field, F32),
            pltpu.VMEM(field, F32),
            pltpu.VMEM((72, 1024), F32),
            pltpu.VMEM((128, C * C), F32),
            pltpu.VMEM((2, 8, 8, C * C), F32),
            pltpu.VMEM(field, BF),
            pltpu.SemaphoreType.DMA((15, N)),
            pltpu.SemaphoreType.DMA((15, N)),
            pltpu.SemaphoreType.DMA((10,)),
        ],
        compiler_params=pltpu.CompilerParams(
            collective_id=0, has_side_effects=True, vmem_limit_bytes=52 * 1024 * 1024
        ),
    )(inputs, cotangent, spectral_weight, point_weight, bias, *consts)
    return grad_input, spectral_grad, pointwise_grad, bias_grad.reshape(C)


def solution(mesh):
    in_specs = (P(None, "row", "col"), P(None, "row", "col"), P(None, "row", "col", None), P(), P())
    out_specs = (P(None, "row", "col"), P(None, "row", "col", None), P(), P())
    return jax.shard_map(body, mesh=mesh, in_specs=in_specs, out_specs=out_specs, check_vma=False)
```

time: 1540 us -> 152 us (0.10)
  waiting for transfers between devices: 1280 us -> 0 us
  Pallas kernels: 0 us -> 140 us
  blocking collectives: 79.7 us -> 0 us
  local copies, waits for them, and re-layouts: 81.9 us -> 11.2 us
  matrix products: 55.3 us -> 0 us
    all_gather x2 -> x0, waiting for transfers between devices: 747 us -> none  [spatial(): gathered = lax.all_gather(blocks, ('row', 'col'), axis=0, tiled=True)]
    reduce_scatter x4 -> x0, waiting for transfers between devices: 538 us -> none  [the longest x2 390 us: spectrum(): lax.psum_scatter(jnp.stack([out_r, out_i], 1), 'row', scatter_dimension=0...]
    pallas_call x0 -> x1, Pallas kernels: none -> 140 us  [body(): pl.pallas_call(kernel, out_shape=(jax.ShapeDtypeStruct(field, BF), jax.Sh...]
    psum x1 -> x0, blocking collectives: 79.7 us -> none  [body(): lax.psum((point_term, bias_term), ('row', 'col'))]
    dot_general x31 -> x0, matrix products: 55.3 us -> none  [the longest x2 6.54 us: spatial(): jnp.einsum('cypk,pkx->cyx', middle, table_x, preferred_element_type=jnp.f...]
    transpose x4 -> x0, local copies, waits for them, and re-layouts: 36.5 us -> none  [the longest x2 18.4 us: spectrum(): jnp.einsum('cyx,xpk->kpcy', field, table, preferred_element_type=jnp.floa...]
  transfers between devices with their start and end apart: 6 -> 0, of which waited for: 6 -> 0; matrix products, arithmetic and copies ran while one was open for 1% -> 0% of each run, Pallas kernels for 0% -> 0%
where the time goes in v1:
time: 152 us
  Pallas kernels  140 us (92%)
  local copies, waits for them, and re-layouts  11.2 us (7%)
    pallas_call x1, Pallas kernels, body(): pl.pallas_call(kernel, out_shape=(jax.ShapeDtypeStruct(field, BF), jax.Sh...  140 us
    unnamed x20, local copies, waits for them, and re-layouts  11.2 us

profile of v1, /device:TPU:1, one launch (start us, length us, event | category | flops | bytes accessed | tf_op | source)
XLA Modules:
  0.0 151.7 jit_solution(17183081273989271193)
XLA Ops:
  0.6 0.0 copy-start
  0.6 1.0 copy-done
  1.7 0.0 copy-start.1
  1.7 1.0 copy-done.1
  2.7 0.0 copy-start.2
  2.7 1.0 copy-done.2
  3.8 0.0 copy-start.3
  3.8 0.9 copy-done.3
  4.7 0.0 copy-start.4
  4.7 0.9 copy-done.4
  5.6 0.0 copy-start.5
  5.6 0.7 copy-done.5
  6.3 0.0 copy-start.6
  6.3 0.7 copy-done.6
  7.0 139.9 %shard_map.138 = (bf16[64,64,128]{2,1,0:T(8,128)(2,1)}, f32[2,8,8,4096]{3,2,1,0:T(8,128)}, f32[64,64]{1,0:T(8,128)S(1)}, f32[1,64]{1,0:T(1,128)S(1)}) custom-call(bf16[64,64,128]{2,1,0:T(8,128)(2,1)} %inp.1, bf16[64,64,128]{2,1,0:T(8,128)(2,1)} %cot.1, bf16[2,8,8,4096]{3,2,1,0:T(8,128)(2,1)} %w.1, bf16[64,64]{1,0:T(8,128)(2,1)S(1)} %copy-done.5, ...), custom_call_target="tpu_custom_call" | custom-call | tf_op jit(solution)/shard_map/pallas_call | solution.py:491
  146.9 0.0 copy-start.7
  146.9 2.4 %copy.19 = bf16[64,64,128]{2,1,0:T(8,128)(2,1)} copy(bf16[64,64,128]{2,1,0:T(8,128)(2,1)} %get-tuple-element.16) | data formatting | bytes 2097152
  149.3 0.0 copy-done.7
  149.3 1.3 copy.20
  150.6 0.6 copy.21
  151.2 0.5 copy.22
Async XLA Ops:
  0.6 1.0 copy-start
  1.7 1.0 copy-start.1
  2.7 1.0 copy-start.2
  3.8 0.9 copy-start.3
  4.7 0.9 copy-start.4
  5.6 0.7 copy-start.5
  6.3 0.7 copy-start.6
  146.9 2.4 %copy-start.7 = (f32[2,8,8,4096]{3,2,1,0:T(8,128)S(1)}, f32[2,8,8,4096]{3,2,1,0:T(8,128)}, u32[]{:S(2)}) copy-start(f32[2,8,8,4096]{3,2,1,0:T(8,128)} %get-tuple-element.17) | copy-start | bytes 6291460

commit v2 on v1

v2 whole, which is shorter than its diff:
```python
import functools
import math

import jax
import jax.numpy as jnp
import ml_dtypes
import numpy as np
from jax import lax
from jax.experimental import pallas as pl
from jax.experimental.pallas import tpu as pltpu
from jax.sharding import PartitionSpec as P

C = 64
K1 = 128
K2 = 128
NY = 1024
NX = 2048
TY = 64
TX = 128
N = 16
SCALE = float(NY * NX) ** (-0.5)
MESH = pl.DeviceIdType.MESH
VMEM_BYTES = 60 * 1024 * 1024
BF = jnp.bfloat16
F32 = jnp.float32

CHIPS = ((1, 2), (0, 1), (0, 3), (1, 1), (0, 2), (1, 0), (1, 3), (0, 0))
COL_ORDER = ((1, 2, 0), (0, 1, 0), (1, 2, 1), (0, 3, 0), (0, 1, 1), (1, 1, 0), (0, 3, 1), (0, 2, 0), (1, 1, 1), (1, 0, 0))
COL_ORDER += ((0, 2, 1), (1, 3, 0), (1, 0, 1), (1, 3, 1), (0, 0, 1))
ROW_ORDER = tuple((x, z) for z in (4, 3, 5, 2, 6, 1, 7, 0) for x in (0, 1) if (x, z) != (0, 0))

X1, Y1, T1, T2, Y2, X2, X3, Y3, T3, T4, Y4, X4, Z1, Z2, Z3 = range(15)


def trig(first, second, total):
    phase = np.mod(first[:, None] * second[None, :], total).astype(np.float32) * np.float32(
        2.0 * math.pi / total
    )
    return np.cos(phase).astype(ml_dtypes.bfloat16), np.sin(phase).astype(ml_dtypes.bfloat16)


@functools.cache
def tables():
    cos, sin = trig(np.arange(K2), np.arange(NX), NX)
    tx = np.stack([cos.reshape(N, 8, NX), -sin.reshape(N, 8, NX)], 1).reshape(2 * K2, 8, NX // 8)
    tx = tx.transpose(1, 0, 2)
    cos, sin = trig(np.arange(K1) - K1 // 2, np.arange(NY), NY)
    ty = np.stack([cos.reshape(K1, N, TY), sin.reshape(K1, N, TY)], 2).reshape(K1, 8, 256)
    ty = ty.transpose(1, 0, 2).reshape(4, 256, 256)
    tyi = np.concatenate([cos, sin], 0).reshape(2 * K1, 4, 256).transpose(1, 0, 2)
    return np.ascontiguousarray(np.concatenate([tx, ty, tyi], 0))


def dot(a, b):
    return lax.dot_general(a, b, (((1,), (0,)), ((), ())), preferred_element_type=F32)


def dot_t(a, b):
    return lax.dot_general(a, b, (((1,), (1,)), ((), ())), preferred_element_type=F32)


def normal_slope(value):
    cumul = 0.5 * (1.0 + lax.erf(value * (1.0 / math.sqrt(2.0))))
    dens = jnp.exp(-0.5 * value * value) * (1.0 / math.sqrt(2.0 * math.pi))
    return cumul + value * dens


def kernel(
    inp, cot, w, pw_hbm, bias_hbm, tab,
    gin, ug, zsum,
    pw, bias, inp_v, cot_v, w_v, tab_v, e1_v, e_v, sel_v,
    xr, yr, tr, xsend, ysend, tsend,
    zsend, zr, f2_v, dz_v, dz2_v, kron_v, zp_v, gz_v, s_v, ug_v, gin_v,
    send_sem, recv_sem, loc_sem,
):
    row = lax.axis_index("row")
    col = lax.axis_index("col")
    col_x, col_y, col_c = lax.div(col, 8), lax.rem(lax.div(col, 2), 4), lax.rem(col, 2)
    lane_lo = lax.broadcasted_iota(jnp.int32, (16, 128), 1) < 64
    mask_j = (lax.broadcasted_iota(jnp.int32, (8, 8, 128), 2) & 7) == lax.broadcasted_iota(
        jnp.int32, (8, 8, 128), 0
    )

    def wrap(i):
        return lax.rem(i, N)

    def remote(src, dst, phase, to, slot, device):
        return pltpu.make_async_remote_copy(
            src_ref=src,
            dst_ref=dst,
            send_sem=send_sem.at[phase, to],
            recv_sem=recv_sem.at[phase, slot],
            device_id=device,
            device_id_type=MESH,
        )

    def wait_recv(dst, phase, slot):
        remote(dst, dst, phase, slot, slot, (row, col)).wait_recv()

    pending = []

    def finish():
        for wait in pending:
            wait()

    def sent(src_of, phase, own):
        def wait():
            @pl.loop(1, N)
            def _(d):
                to = wrap(own + d)
                remote(src_of(to), src_of(to), phase, to, to, (row, col)).wait_send()

        pending.append(wait)

    def row_partner(x, z):
        z = jnp.where(col_c == 0, z, 8 - z)
        return 8 * (lax.div(row, 8) ^ x) + lax.rem(lax.rem(row, 8) + z, 8)

    def col_partner(x, y, c, own_core):
        y = jnp.where(own_core == 0, y, 4 - y)
        return 8 * (col_x ^ x) + 2 * lax.rem(col_y + y, 4) + (col_c ^ c)

    def send_row(src_of, dst, phase, slot):
        for x, z in ROW_ORDER:
            r = row_partner(x, z)
            remote(src_of(r), dst.at[slot], phase, r, slot, (r, col)).start()

        sent(src_of, phase, row)

    def send_block(src, dst, m, phase):
        remote(src, dst.at[col], phase, m, col, (row, m)).start()

    def send_col(src_of, dst, phase):
        for x, y, c in COL_ORDER:
            m = col_partner(x, y, c, col_c)
            send_block(src_of(m), dst, m, phase)

        sent(src_of, phase, col)

    def wait_all(dst, phase, own):
        @pl.loop(1, N)
        def _(d):
            slot = wrap(own + d)
            wait_recv(dst.at[slot], phase, slot)

    block = wrap(row + col)
    top = row == 0

    def send_t(src, dst, phase, to_modes):
        own = row if to_modes else col

        @pl.loop(0, N)
        def _(i):
            @pl.when(jnp.logical_not(jnp.logical_and(top, i == own)))
            def _():
                if to_modes:
                    remote(src.at[i], dst.at[col], phase, i, col, (i, block)).start()
                else:
                    target = (wrap(col + N - i), i)
                    remote(src.at[i], dst.at[row], phase, i, row, target).start()

        @pl.when(top)
        def _():
            dst[col if to_modes else row] = src[own]

        def wait():
            @pl.loop(0, N)
            def _(i):
                @pl.when(jnp.logical_not(jnp.logical_and(top, i == own)))
                def _():
                    remote(src.at[i], src.at[i], phase, i, i, (row, col)).wait_send()

        pending.append(wait)

    def wait_t(dst, phase, to_modes):
        own = col if to_modes else row

        @pl.loop(0, N)
        def _(i):
            @pl.when(jnp.logical_not(jnp.logical_and(top, i == own)))
            def _():
                wait_recv(dst.at[i], phase, i)

    barrier = pltpu.get_barrier_semaphore()

    @pl.loop(1, N)
    def _(d):
        pl.semaphore_signal(barrier, inc=1, device_id=(row, wrap(col + d)), device_id_type=MESH)
        pl.semaphore_signal(barrier, inc=1, device_id=(wrap(row + d), col), device_id_type=MESH)

    @pl.loop(0, N)
    def _(i):
        @pl.when(jnp.logical_not(jnp.logical_and(top, i == row)))
        def _():
            pl.semaphore_signal(barrier, inc=1, device_id=(i, block), device_id_type=MESH)

        @pl.when(jnp.logical_not(jnp.logical_and(top, i == col)))
        def _():
            target = (wrap(col + N - i), i)
            pl.semaphore_signal(barrier, inc=1, device_id=target, device_id_type=MESH)

    loads = [
        pltpu.make_async_copy(src, dst, loc_sem.at[i])
        for i, (src, dst) in enumerate(
            [
                (pw_hbm, pw),
                (bias_hbm, bias),
                (inp, inp_v),
                (tab, tab_v),
                (inp.at[pl.ds(4 * col, 4)], xr.at[0, col]),
                (w, w_v),
                (cot, cot_v),
            ]
        )
    ]
    for load in loads:
        load.start()
    pl.semaphore_wait(barrier, jnp.where(top, 4 * N - 4, 4 * N - 2))

    send_col(lambda m: inp.at[pl.ds(4 * m, 4)], xr.at[0], X1)

    def pack(src, dst):
        for b in range(4):
            dst[:, 128 * b : 128 * b + 128] = src[:, 16 * b : 16 * b + 16, :].reshape(1024, 128)

    def build_kron(which):
        @pl.loop(0, 4)
        def _(i):
            rows = pl.ds(pl.multiple_of(256 * i, 256), 256)
            part = (dot_t if which == 0 else dot)(sel_v[rows, :], pw[...]).astype(BF)
            for j in range(4):
                full = dot_t(part, sel_v[256 * j : 256 * j + 256, :])
                same = (lax.broadcasted_iota(jnp.int32, (256, 256), 0) & 15) == (
                    lax.broadcasted_iota(jnp.int32, (256, 256), 1) & 15
                )
                kron_v[which, rows, 256 * j : 256 * j + 256] = jnp.where(same, full, 0.0).astype(BF)

    def apply_kron(which, src, dst):
        @pl.loop(0, 4)
        def _(i):
            rows = pl.ds(pl.multiple_of(256 * i, 256), 256)
            out = pl.ds(pl.multiple_of(16 * i, 16), 16)
            for h in range(2):
                res = dot(kron_v[which, rows, :], src[:, 256 * h : 256 * h + 256])
                for t in range(2):
                    y = 32 * h + 16 * t
                    dst[out, y : y + 16, :] = res[:, 128 * t : 128 * t + 128].reshape(16, 16, 128)

    def forward_x(src, phase, dst):
        acc = jnp.zeros((256, 256), F32)
        for x, y in CHIPS:
            chip = 4 * (col_x ^ x) + lax.rem(col_y + y, 4)
            blocks = []
            for c in range(2):
                slot = 2 * chip + c

                @pl.when(slot != col)
                def _(slot=slot):
                    wait_recv(src.at[slot], phase, slot)

                blocks.append(src[slot].reshape(256, 128))
            acc = acc + dot_t(tab_v[chip], jnp.concatenate(blocks, 1))
        dst[...] = acc.astype(BF).reshape(N, 16, 256)

    def forward_y(src, dst):
        acc = jnp.zeros((K1, 64), F32)
        for q in range(4):
            parts = []
            for t in range(4):
                b = src[4 * q + t].astype(F32)
                jb = jnp.concatenate([b[8:16], -b[0:8]], 0)
                rows = []
                for h in range(2):
                    bh = b[:, 128 * h : 128 * h + 128]
                    jh = jb[:, 128 * h : 128 * h + 128]
                    rows.append(jnp.where(lane_lo, bh, pltpu.roll(jh, 64, 1)))
                    rows.append(jnp.where(lane_lo, pltpu.roll(bh, 64, 1), jh))
                parts.append(jnp.concatenate(rows, 0).astype(BF))
            for h in range(2):
                table = tab_v[8 + q, 128 * h : 128 * h + 128, :]
                acc = acc + dot_t(table, jnp.concatenate(parts[2 * h : 2 * h + 2], 1))
        res = (acc * SCALE).astype(BF).astype(F32)
        res = res.reshape(N, 8, 64)
        dst[...] = jnp.concatenate([res[:, 0:4], res[:, 4:8]], 2)

    def unpack_t(src):
        x = src[...]
        x = jnp.concatenate([x, pltpu.roll(x, 64, 2)], 1)
        return x.reshape(128, 128).T

    def to_modes(src):
        xt = unpack_t(src)
        rows = []
        for ri in range(2):
            cols = []
            for c in range(4):
                at = (2 * c + ri) * 8
                tile = xt[at : at + 8]
                cols.append(jnp.where(mask_j, tile[None], 0.0).reshape(64, 128))
            rows.append(jnp.concatenate(cols, 1))
        return dot(jnp.concatenate(rows, 0).astype(BF), e1_v[...])

    def from_modes(spec, dst):
        full = dot_t(spec.astype(BF), e1_v[...])
        tiles = []
        for c in range(4):
            for ri in range(2):
                part = full[64 * ri : 64 * ri + 64, 128 * c : 128 * c + 128].reshape(8, 8, 128)
                tiles.append(jnp.sum(jnp.where(mask_j, part, 0.0), axis=0))
        xt = jnp.concatenate(tiles + [jnp.zeros((64, 128), F32)], 0)
        x = xt.T.reshape(N, 8, 128)
        dst[...] = jnp.concatenate([x[:, 0:4, 0:64], x[:, 4:8, 0:64]], 2)

    def inverse_y(src, dst):
        ht = unpack_t(src)
        first, second = [], []
        for c in range(4):
            hr, hi = ht[16 * c : 16 * c + 8], ht[16 * c + 8 : 16 * c + 16]
            first += [hr, hi]
            second += [-hi, hr]
        h = jnp.concatenate([jnp.concatenate(first, 0), jnp.concatenate(second, 0)], 1).astype(BF)
        d = jnp.concatenate([dot(h, tab_v[12 + i]) for i in range(4)], 1)
        for a in range(8):
            for p in range(2):
                t0 = d[32 * p : 32 * p + 16, 128 * a : 128 * a + 128]
                t1 = d[32 * p + 16 : 32 * p + 32, 128 * a : 128 * a + 128]
                at = slice(128 * p, 128 * p + 128)
                dst[2 * a, :, at] = jnp.where(lane_lo, t0, pltpu.roll(t1, 64, 1)).astype(BF)
                dst[2 * a + 1, :, at] = jnp.where(lane_lo, pltpu.roll(t0, 64, 1), t1).astype(BF)

    def inverse_x(src, out, dst, phase):
        yt = src[...].reshape(256, 256).astype(F32).T.astype(BF)
        late = None
        for x, y in CHIPS:
            chip = 4 * (col_x ^ x) + lax.rem(col_y + jnp.where(col_c == 0, y, 4 - y), 4)
            res = (dot(yt, tab_v[chip]) * SCALE).astype(BF)
            for c in range(2):
                out[2 * chip + c] = res[:, 128 * c : 128 * c + 128].reshape(4, TY, TX)
            m = 2 * chip + col_c
            if (x, y) != (0, 0):
                send_block(out.at[m], dst, m, phase)
            else:
                dst[m] = out[m]
            if late is not None:
                send_block(out.at[late], dst, late, phase)
            late = m ^ 1
        send_block(out.at[late], dst, late, phase)

        sent(lambda m: out.at[m], phase, col)

    lane = lax.broadcasted_iota(jnp.int32, (1024, 64), 1)
    first = lax.broadcasted_iota(jnp.int32, (1024, 64), 0)
    sel_v[...] = jnp.where((first >> 4) == lane, 1.0, 0.0).astype(BF)
    zsend[...] = jnp.zeros_like(zsend)
    loads[0].wait()
    build_kron(0)
    loads[2].wait()
    pack(inp_v, f2_v)
    apply_kron(0, f2_v, zp_v)
    first, lane = first[0:512], lane[0:512]
    at = (((first >> 3) & 15) << 2) + (first >> 7)
    e1_v[...] = jnp.where(at == lane, 1.0, 0.0).astype(BF)

    @pl.loop(0, 8)
    def _(i):
        channel = (lax.broadcasted_iota(jnp.int32, (64, 512), 1) >> 6) + 8 * i
        own = lax.broadcasted_iota(jnp.int32, (64, 512), 0)
        at = pl.ds(pl.multiple_of(i * 512, 512), 512)
        e_v[:, at] = jnp.where(channel == own, 1.0, 0.0).astype(BF)

    loads[3].wait()
    loads[4].wait()
    forward_x(xr.at[0], X1, ysend.at[0])
    send_row(lambda r: ysend.at[0, wrap(r + col)], yr.at[0], Y1, row)
    yr[0, row] = ysend[0, block]
    build_kron(1)
    wait_all(yr.at[0], Y1, row)
    forward_y(yr.at[0], tsend.at[0])
    send_t(tsend.at[0], tr.at[0], T1, True)
    loads[5].wait()
    wait_t(tr.at[0], T1, True)

    u = to_modes(tr.at[0])
    ug_v[0] = u
    u = u.astype(BF)

    def fold(t):
        return t[:, 0:128] + t[:, 128:256] + t[:, 256:384] + t[:, 384:512]

    def mix(i, carry):
        sr, si = carry
        at = pl.ds(pl.multiple_of(i * 512, 512), 512)
        ue = dot(u, e_v[:, at])
        ur, ui = ue[0:64], ue[64:128]
        wr = w_v[0, :, :, at].astype(F32).reshape(64, 512)
        wi = w_v[1, :, :, at].astype(F32).reshape(64, 512)
        return sr + fold(wr * ur - wi * ui), si + fold(wr * ui + wi * ur)

    zero = jnp.zeros((64, 128), F32)
    sr, si = lax.fori_loop(0, 8, mix, (zero, zero))
    both = jnp.concatenate([sr, si], 0)
    both = both + pltpu.roll(both, 64, 1)
    from_modes(both[:, 0:64], tsend.at[1])
    send_t(tsend.at[1], tr.at[1], T2, False)

    wait_t(tr.at[1], T2, False)
    inverse_y(tr.at[1], ysend.at[1])
    send_row(lambda r: ysend.at[1, r], yr.at[1], Y2, block)
    yr[1, block] = ysend[1, row]
    wait_all(yr.at[1], Y2, block)
    inverse_x(yr.at[1], xsend.at[0], xr.at[1], X2)

    loads[1].wait()
    loads[6].wait()
    def slope(m):
        for c in range(4):
            z = xr[1, m, c].astype(F32) + zp_v[4 * m + c] + bias[4 * m + c]
            dz = cot_v[4 * m + c].astype(F32) * normal_slope(z)
            dz_v[4 * m + c] = dz.astype(BF)

    slope(col)
    xr[2, col] = dz_v[pl.ds(4 * col, 4)]
    for x, y, c in COL_ORDER:
        m = col_partner(x, 4 - y, c, col_c ^ c)
        wait_recv(xr.at[1, m], X2, m)
        slope(m)
        send_block(dz_v.at[pl.ds(4 * m, 4)], xr.at[2], m, X3)
    sent(lambda m: dz_v.at[pl.ds(4 * m, 4)], X3, col)

    pack(dz_v, dz2_v)

    @pl.loop(0, 4)
    def _(o):
        cols = pl.ds(pl.multiple_of(256 * o, 256), 256)
        dzo = dz2_v[cols, :]
        same = (lax.broadcasted_iota(jnp.int32, (256, 256), 0) & 15) == (
            lax.broadcasted_iota(jnp.int32, (256, 256), 1) & 15
        )
        for i in range(4):
            prod = dot_t(f2_v[256 * i : 256 * i + 256, :], dzo)
            prod = jnp.where(same, prod, 0.0).reshape(16, 16, 256)
            s_v[16 * i : 16 * i + 16, cols] = jnp.sum(prod, axis=1)
        s_v[64:72, cols] = dot_t(jnp.ones((16, 512), BF), dzo)[0:8]

    terms = s_v[...]
    high = terms.astype(BF)
    low = (terms - high.astype(F32)).astype(BF)
    terms = dot(high, sel_v[...]) + dot(low, sel_v[...])
    zsend[:, 0:4, 0:64] = terms[0:64].reshape(N, 4, 64)
    zsend[0, 4:5, 0:64] = terms[64:65]
    send_col(lambda m: zsend.at[m], zr.at[0], Z1)
    zr[0, col] = zsend[col]
    apply_kron(1, dz2_v, gz_v)

    forward_x(xr.at[2], X3, ysend.at[2])
    send_row(lambda r: ysend.at[2, wrap(r + col)], yr.at[2], Y3, row)
    yr[2, row] = ysend[2, block]
    wait_all(yr.at[2], Y3, row)
    forward_y(yr.at[2], tsend.at[2])
    send_t(tsend.at[2], tr.at[2], T3, True)
    wait_all(zr.at[0], Z1, col)
    zr[3, 0] = jnp.sum(zr[0], axis=0)
    send_row(lambda r: zr.at[3, 0], zr.at[1], Z2, row)
    zr[1, row] = zr[3, 0]
    wait_t(tr.at[2], T3, True)

    g = to_modes(tr.at[2])
    ug_v[1] = g
    g = jnp.concatenate([g, g], 1)
    gr, gi = g[0:64], g[64:128]
    gr4, gi4 = jnp.concatenate([gr] * 4, 1), jnp.concatenate([gi] * 4, 1)

    def mix_back(i, acc):
        at = pl.ds(pl.multiple_of(i * 512, 512), 512)
        wr = w_v[0, :, :, at].astype(F32).reshape(64, 512)
        wi = w_v[1, :, :, at].astype(F32).reshape(64, 512)
        both = jnp.concatenate([wr * gr4 + wi * gi4, wr * gi4 - wi * gr4], 0).astype(BF)
        return acc + dot_t(both, e_v[:, at])

    du = lax.fori_loop(0, 8, mix_back, jnp.zeros((128, 64), F32))
    from_modes(du, tsend.at[3])
    send_t(tsend.at[3], tr.at[3], T4, False)

    wait_all(zr.at[1], Z2, row)
    zr[3, 1] = jnp.sum(zr[1], axis=0)
    send_col(lambda m: zr.at[3, 1], zr.at[2], Z3)
    zr[2, col] = zr[3, 1]
    out_ug = pltpu.make_async_copy(ug_v, ug, loc_sem.at[0])
    out_ug.start()

    wait_t(tr.at[3], T4, False)
    inverse_y(tr.at[3], ysend.at[3])
    send_row(lambda r: ysend.at[3, r], yr.at[3], Y4, block)
    yr[3, block] = ysend[3, row]
    wait_all(zr.at[2], Z3, col)
    out_z = pltpu.make_async_copy(zr.at[2], zsum, loc_sem.at[2])
    out_z.start()
    pending.append(out_z.wait)
    wait_all(yr.at[3], Y4, block)
    inverse_x(yr.at[3], xsend.at[1], xr.at[3], X4)
    def finish_block(m):
        at = pl.ds(4 * m, 4)
        gin_v[at] = (xr[3, m].astype(F32) + gz_v[at]).astype(BF)

    finish_block(col)
    for x, y, c in COL_ORDER:
        m = col_partner(x, 4 - y, c, col_c ^ c)
        wait_recv(xr.at[3, m], X4, m)
        finish_block(m)

    out_gin = pltpu.make_async_copy(gin_v, gin, loc_sem.at[1])
    out_gin.start()

    pending.append(out_ug.wait)
    pending.append(out_gin.wait)
    finish()


def last_kernel(gin, ug, zsum, gin_out, sg, pg, bg):
    step = pl.program_id(0)
    gin_out[...] = gin[...]

    @pl.when(step == 0)
    def _():
        pg[...] = zsum[:, 0:4, 0:64].reshape(C, C) * SCALE
        bg[...] = zsum[0, 4:5, 0:64] * SCALE

    channel = (lax.broadcasted_iota(jnp.int32, (64, 1024), 1) >> 6) + 16 * step
    own = lax.broadcasted_iota(jnp.int32, (64, 1024), 0)
    ue = dot(ug[0].astype(BF), jnp.where(channel == own, 1.0, 0.0).astype(BF))
    g = jnp.concatenate([ug[1]] * 16, 1)
    ur, ui, gr, gi = ue[0:64], ue[64:128], g[0:64], g[64:128]
    sg[0] = (gr * ur + gi * ui).reshape(8, 8, 1024)
    sg[1] = (gi * ur - gr * ui).reshape(8, 8, 1024)


def body(inputs, cotangent, spectral_weight, point_weight, bias):
    any_spec = pl.BlockSpec(memory_space=pl.ANY)
    field = (C, TY, TX)
    table = jnp.asarray(tables())
    grad_input, modes, sums = pl.pallas_call(
        kernel,
        out_shape=(
            jax.ShapeDtypeStruct(field, BF),
            jax.ShapeDtypeStruct((2, 128, C), F32),
            jax.ShapeDtypeStruct((N, 8, 128), F32),
        ),
        in_specs=[any_spec] * 6,
        out_specs=(any_spec, any_spec, any_spec),
        scratch_shapes=[
            pltpu.VMEM((C, C), BF),
            pltpu.SMEM((C,), F32),
            pltpu.VMEM(field, BF),
            pltpu.VMEM(field, BF),
            pltpu.VMEM((2, 8, 8, C * C), BF),
            pltpu.VMEM(table.shape, BF),
            pltpu.VMEM((512, 64), BF),
            pltpu.VMEM((64, C * C), BF),
            pltpu.VMEM((1024, 64), BF),
            pltpu.VMEM((4, N, 4, TY, TX), BF),
            pltpu.VMEM((4, N, 16, 256), BF),
            pltpu.VMEM((4, N, 4, 128), F32),
            pltpu.VMEM((2, N, 4, TY, TX), BF),
            pltpu.VMEM((4, N, 16, 256), BF),
            pltpu.VMEM((4, N, 4, 128), F32),
            pltpu.VMEM((N, 8, 128), F32),
            pltpu.VMEM((4, N, 8, 128), F32),
            pltpu.VMEM((1024, 512), BF),
            pltpu.VMEM(field, BF),
            pltpu.VMEM((1024, 512), BF),
            pltpu.VMEM((2, 1024, 1024), BF),
            pltpu.VMEM(field, F32),
            pltpu.VMEM(field, F32),
            pltpu.VMEM((72, 1024), F32),
            pltpu.VMEM((2, 128, C), F32),
            pltpu.VMEM(field, BF),
            pltpu.SemaphoreType.DMA((15, N)),
            pltpu.SemaphoreType.DMA((15, N)),
            pltpu.SemaphoreType.DMA((10,)),
        ],
        compiler_params=pltpu.CompilerParams(
            collective_id=0, has_side_effects=True, vmem_limit_bytes=VMEM_BYTES
        ),
    )(inputs, cotangent, spectral_weight, point_weight, bias, table)
    channels = pl.BlockSpec((C // 4, TY, TX), lambda i: (i, 0, 0))
    whole = lambda shape: pl.BlockSpec(shape, lambda i: (0,) * len(shape))
    grad_input, spectral_grad, pointwise_grad, bias_grad = pl.pallas_call(
        last_kernel,
        grid=(4,),
        out_shape=(
            jax.ShapeDtypeStruct(field, BF),
            jax.ShapeDtypeStruct((2, 8, 8, C * C), F32),
            jax.ShapeDtypeStruct((C, C), F32),
            jax.ShapeDtypeStruct((1, C), F32),
        ),
        in_specs=[channels, whole((2, 128, C)), whole((N, 8, 128))],
        out_specs=(
            channels,
            pl.BlockSpec((2, 8, 8, 1024), lambda i: (0, 0, 0, i)),
            whole((C, C)),
            whole((1, C)),
        ),
    )(grad_input, modes, sums)
    return grad_input, spectral_grad, pointwise_grad, bias_grad.reshape(C)


def solution(mesh):
    in_specs = (P(None, "row", "col"), P(None, "row", "col"), P(None, "row", "col", None), P(), P())
    out_specs = (P(None, "row", "col"), P(None, "row", "col", None), P(), P())
    return jax.shard_map(body, mesh=mesh, in_specs=in_specs, out_specs=out_specs, check_vma=False)
```

time: 152 us -> 138 us (0.908)
  local copies, waits for them, and re-layouts: 11.2 us -> 0 us
  Pallas kernels: 140 us -> 137 us
    unnamed x20 -> x0, local copies, waits for them, and re-layouts: 11.2 us -> none
    pallas_call x1, Pallas kernels: 140 us -> 133 us  [body(): pl.pallas_call(kernel, out_shape=(jax.ShapeDtypeStruct(field, BF), jax.Sh...]
    pallas_call x0 -> x1, Pallas kernels: none -> 4.03 us  [body(): pl.pallas_call(last_kernel, grid=(4,), out_shape=(jax.ShapeDtypeStruct(fi...]
where the time goes in v2:
time: 138 us
  Pallas kernels  137 us (99%)
    pallas_call x1, Pallas kernels, body(): pl.pallas_call(kernel, out_shape=(jax.ShapeDtypeStruct(field, BF), jax.Sh...  133 us
    pallas_call x1, Pallas kernels, body(): pl.pallas_call(last_kernel, grid=(4,), out_shape=(jax.ShapeDtypeStruct(fi...  4.03 us

profile of v2, /device:TPU:1, one launch (start us, length us, event | category | flops | bytes accessed | tf_op | source)
XLA Modules:
  0.0 138.0 jit_solution(7941677692941532762)
XLA Ops:
  0.6 133.3 %shard_map.93 = (bf16[64,64,128]{2,1,0:T(8,128)(2,1)}, f32[2,128,64]{2,1,0:T(8,128)}, f32[16,8,128]{2,1,0:T(8,128)}) custom-call(bf16[64,64,128]{2,1,0:T(8,128)(2,1)} %inp.1, bf16[64,64,128]{2,1,0:T(8,128)(2,1)} %cot.1, bf16[2,8,8,4096]{3,2,1,0:T(8,128)(2,1)} %w.1, bf16[64,64]{1,0:T(8,128)(2,1)} %pw_hbm.1, f32[64]{0:T(128)} %bias_hbm.1, ...), custom_call_target="tpu_custom_call" | custom-call | tf_op jit(solution)/shard_map/pallas_call | solution.py:541
  133.9 4.0 %shard_map.94 = (bf16[64,64,128]{2,1,0:T(8,128)(2,1)}, f32[2,8,8,4096]{3,2,1,0:T(8,128)}, f32[64,64]{1,0:T(8,128)}, f32[1,64]{1,0:T(1,128)}) custom-call(bf16[64,64,128]{2,1,0:T(8,128)(2,1)} %get-tuple-element.11.gin, f32[2,128,64]{2,1,0:T(8,128)} %get-tuple-element.12.ug, f32[16,8,128]{2,1,0:T(8,128)} %get-tuple-element.13.zsum), custom_call_target="tpu_custom_call" | custom-call | tf_op jit(solution)/shard_map/pallas_call | solution.py:587

commit v3 on v2

--- a/solution.py
+++ b/solution.py
@@ -84,18 +84,24 @@
     def wrap(i):
         return lax.rem(i, N)
 
-    def remote(src, dst, phase, to, slot, device):
+    def remote(src, dst, phase, slot, device):
         return pltpu.make_async_remote_copy(
             src_ref=src,
             dst_ref=dst,
-            send_sem=send_sem.at[phase, to],
+            send_sem=send_sem.at[phase],
             recv_sem=recv_sem.at[phase, slot],
             device_id=device,
             device_id_type=MESH,
         )
 
-    def wait_recv(dst, phase, slot):
-        remote(dst, dst, phase, slot, slot, (row, col)).wait_recv()
+    def wait_recv(dst, phase, slot=0):
+        remote(dst, dst, phase, slot, (row, col)).wait_recv()
+
+    def wait_sent(like, phase):
+        remote(like, like, phase, 0, (row, col)).wait_send()
+
+    def keep(src, dst, phase):
+        pltpu.make_async_copy(src, dst, recv_sem.at[phase, 0]).start()
 
     pending = []
 
@@ -103,14 +109,8 @@
         for wait in pending:
             wait()
 
-    def sent(src_of, phase, own):
-        def wait():
-            @pl.loop(1, N)
-            def _(d):
-                to = wrap(own + d)
-                remote(src_of(to), src_of(to), phase, to, to, (row, col)).wait_send()
-
-        pending.append(wait)
+    def sent(like, phase):
+        pending.append(lambda: wait_sent(like, phase))
 
     def row_partner(x, z):
         z = jnp.where(col_c == 0, z, 8 - z)
@@ -120,66 +120,61 @@
         y = jnp.where(own_core == 0, y, 4 - y)
         return 8 * (col_x ^ x) + 2 * lax.rem(col_y + y, 4) + (col_c ^ c)
 
-    def send_row(src_of, dst, phase, slot):
+    def ordered(k):
+        words = [0, 0]
+        for i, (x, y, c) in enumerate(COL_ORDER):
+            words[i // 8] |= (8 * x + 2 * y + c) << (4 * (i % 8))
+        words = [w - (1 << 32) if w >> 31 else w for w in words]
+        code = (jnp.where(k < 8, words[0], words[1]) >> (4 * lax.rem(k, 8))) & 15
+        return code >> 3, (code >> 1) & 3, code & 1
+
+    def send_block(src, dst, m, phase):
+        remote(src, dst.at[col], phase, col, (row, m)).start()
+
+    def send_row(src_of, dst, phase, slot, like):
         for x, z in ROW_ORDER:
             r = row_partner(x, z)
-            remote(src_of(r), dst.at[slot], phase, r, slot, (r, col)).start()
-
-        sent(src_of, phase, row)
-
-    def send_block(src, dst, m, phase):
-        remote(src, dst.at[col], phase, m, col, (row, m)).start()
-
-    def send_col(src_of, dst, phase):
+            remote(src_of(r), dst.at[slot], phase, 0, (r, col)).start()
+        keep(src_of(row), dst.at[slot], phase)
+        sent(like, phase)
+
+    def send_col(src_of, dst, phase, like):
         for x, y, c in COL_ORDER:
             m = col_partner(x, y, c, col_c)
-            send_block(src_of(m), dst, m, phase)
-
-        sent(src_of, phase, col)
-
-    def wait_all(dst, phase, own):
-        @pl.loop(1, N)
-        def _(d):
-            slot = wrap(own + d)
-            wait_recv(dst.at[slot], phase, slot)
+            remote(src_of(m), dst.at[col], phase, 0, (row, m)).start()
+        keep(src_of(col), dst.at[col], phase)
+        sent(like, phase)
 
     block = wrap(row + col)
     top = row == 0
 
     def send_t(src, dst, phase, to_modes):
         own = row if to_modes else col
+        slot = col if to_modes else row
 
         @pl.loop(0, N)
         def _(i):
-            @pl.when(jnp.logical_not(jnp.logical_and(top, i == own)))
+            target = (i, block) if to_modes else (wrap(col + N - i), i)
+            is_own = jnp.logical_and(top, i == own)
+
+            @pl.when(jnp.logical_not(is_own))
             def _():
-                if to_modes:
-                    remote(src.at[i], dst.at[col], phase, i, col, (i, block)).start()
-                else:
-                    target = (wrap(col + N - i), i)
-                    remote(src.at[i], dst.at[row], phase, i, row, target).start()
-
-        @pl.when(top)
-        def _():
-            dst[col if to_modes else row] = src[own]
+                remote(src.at[i], dst.at[slot], phase, 0, target).start()
+
+            @pl.when(is_own)
+            def _():
+                keep(src.at[i], dst.at[slot], phase)
 
         def wait():
-            @pl.loop(0, N)
-            def _(i):
-                @pl.when(jnp.logical_not(jnp.logical_and(top, i == own)))
-                def _():
-                    remote(src.at[i], src.at[i], phase, i, i, (row, col)).wait_send()
+            @pl.when(top)
+            def _():
+                wait_sent(src.at[pl.ds(0, N - 1)], phase)
+
+            @pl.when(jnp.logical_not(top))
+            def _():
+                wait_sent(src, phase)
 
         pending.append(wait)
-
-    def wait_t(dst, phase, to_modes):
-        own = col if to_modes else row
-
-        @pl.loop(0, N)
-        def _(i):
-            @pl.when(jnp.logical_not(jnp.logical_and(top, i == own)))
-            def _():
-                wait_recv(dst.at[i], phase, i)
 
     barrier = pltpu.get_barrier_semaphore()
 
@@ -187,17 +182,6 @@
     def _(d):
         pl.semaphore_signal(barrier, inc=1, device_id=(row, wrap(col + d)), device_id_type=MESH)
         pl.semaphore_signal(barrier, inc=1, device_id=(wrap(row + d), col), device_id_type=MESH)
-
-    @pl.loop(0, N)
-    def _(i):
-        @pl.when(jnp.logical_not(jnp.logical_and(top, i == row)))
-        def _():
-            pl.semaphore_signal(barrier, inc=1, device_id=(i, block), device_id_type=MESH)
-
-        @pl.when(jnp.logical_not(jnp.logical_and(top, i == col)))
-        def _():
-            target = (wrap(col + N - i), i)
-            pl.semaphore_signal(barrier, inc=1, device_id=target, device_id_type=MESH)
 
     loads = [
         pltpu.make_async_copy(src, dst, loc_sem.at[i])
@@ -215,9 +199,12 @@
     ]
     for load in loads:
         load.start()
-    pl.semaphore_wait(barrier, jnp.where(top, 4 * N - 4, 4 * N - 2))
-
-    send_col(lambda m: inp.at[pl.ds(4 * m, 4)], xr.at[0], X1)
+    pl.semaphore_wait(barrier, 2 * N - 2)
+
+    for x, y, c in COL_ORDER:
+        m = col_partner(x, y, c, col_c)
+        send_block(inp.at[pl.ds(4 * m, 4)], xr.at[0], m, X1)
+    sent(inp.at[pl.ds(0, 4 * N - 4)], X1)
 
     def pack(src, dst):
         for b in range(4):
@@ -346,7 +333,7 @@
             late = m ^ 1
         send_block(out.at[late], dst, late, phase)
 
-        sent(lambda m: out.at[m], phase, col)
+        sent(out.at[pl.ds(0, N - 1)], phase)
 
     lane = lax.broadcasted_iota(jnp.int32, (1024, 64), 1)
     first = lax.broadcasted_iota(jnp.int32, (1024, 64), 0)
@@ -371,14 +358,13 @@
     loads[3].wait()
     loads[4].wait()
     forward_x(xr.at[0], X1, ysend.at[0])
-    send_row(lambda r: ysend.at[0, wrap(r + col)], yr.at[0], Y1, row)
-    yr[0, row] = ysend[0, block]
+    send_row(lambda r: ysend.at[0, wrap(r + col)], yr.at[0], Y1, row, ysend.at[0, pl.ds(0, N - 1)])
     build_kron(1)
-    wait_all(yr.at[0], Y1, row)
+    wait_recv(yr.at[0], Y1)
     forward_y(yr.at[0], tsend.at[0])
     send_t(tsend.at[0], tr.at[0], T1, True)
     loads[5].wait()
-    wait_t(tr.at[0], T1, True)
+    wait_recv(tr.at[0], T1)
 
     u = to_modes(tr.at[0])
     ug_v[0] = u
@@ -403,11 +389,10 @@
     from_modes(both[:, 0:64], tsend.at[1])
     send_t(tsend.at[1], tr.at[1], T2, False)
 
-    wait_t(tr.at[1], T2, False)
+    wait_recv(tr.at[1], T2)
     inverse_y(tr.at[1], ysend.at[1])
-    send_row(lambda r: ysend.at[1, r], yr.at[1], Y2, block)
-    yr[1, block] = ysend[1, row]
-    wait_all(yr.at[1], Y2, block)
+    send_row(lambda r: ysend.at[1, r], yr.at[1], Y2, block, ysend.at[1, pl.ds(0, N - 1)])
+    wait_recv(yr.at[1], Y2)
     inverse_x(yr.at[1], xsend.at[0], xr.at[1], X2)
 
     loads[1].wait()
@@ -420,12 +405,16 @@
 
     slope(col)
     xr[2, col] = dz_v[pl.ds(4 * col, 4)]
-    for x, y, c in COL_ORDER:
+
+    @pl.loop(0, N - 1)
+    def _(k):
+        x, y, c = ordered(k)
         m = col_partner(x, 4 - y, c, col_c ^ c)
         wait_recv(xr.at[1, m], X2, m)
         slope(m)
         send_block(dz_v.at[pl.ds(4 * m, 4)], xr.at[2], m, X3)
-    sent(lambda m: dz_v.at[pl.ds(4 * m, 4)], X3, col)
+
+    sent(dz_v.at[pl.ds(0, 4 * N - 4)], X3)
 
     pack(dz_v, dz2_v)
 
@@ -448,21 +437,18 @@
     terms = dot(high, sel_v[...]) + dot(low, sel_v[...])
     zsend[:, 0:4, 0:64] = terms[0:64].reshape(N, 4, 64)
     zsend[0, 4:5, 0:64] = terms[64:65]
-    send_col(lambda m: zsend.at[m], zr.at[0], Z1)
-    zr[0, col] = zsend[col]
+    send_col(lambda m: zsend.at[m], zr.at[0], Z1, zsend.at[pl.ds(0, N - 1)])
     apply_kron(1, dz2_v, gz_v)
 
     forward_x(xr.at[2], X3, ysend.at[2])
-    send_row(lambda r: ysend.at[2, wrap(r + col)], yr.at[2], Y3, row)
-    yr[2, row] = ysend[2, block]
-    wait_all(yr.at[2], Y3, row)
+    send_row(lambda r: ysend.at[2, wrap(r + col)], yr.at[2], Y3, row, ysend.at[2, pl.ds(0, N - 1)])
+    wait_recv(yr.at[2], Y3)
     forward_y(yr.at[2], tsend.at[2])
     send_t(tsend.at[2], tr.at[2], T3, True)
-    wait_all(zr.at[0], Z1, col)
+    wait_recv(zr.at[0], Z1)
     zr[3, 0] = jnp.sum(zr[0], axis=0)
-    send_row(lambda r: zr.at[3, 0], zr.at[1], Z2, row)
-    zr[1, row] = zr[3, 0]
-    wait_t(tr.at[2], T3, True)
+    send_row(lambda r: zr.at[3, 0], zr.at[1], Z2, row, zsend.at[pl.ds(0, N - 1)])
+    wait_recv(tr.at[2], T3)
 
     g = to_modes(tr.at[2])
     ug_v[1] = g
@@ -481,29 +467,30 @@
     from_modes(du, tsend.at[3])
     send_t(tsend.at[3], tr.at[3], T4, False)
 
-    wait_all(zr.at[1], Z2, row)
+    wait_recv(zr.at[1], Z2)
     zr[3, 1] = jnp.sum(zr[1], axis=0)
-    send_col(lambda m: zr.at[3, 1], zr.at[2], Z3)
-    zr[2, col] = zr[3, 1]
+    send_col(lambda m: zr.at[3, 1], zr.at[2], Z3, zsend.at[pl.ds(0, N - 1)])
     out_ug = pltpu.make_async_copy(ug_v, ug, loc_sem.at[0])
     out_ug.start()
 
-    wait_t(tr.at[3], T4, False)
+    wait_recv(tr.at[3], T4)
     inverse_y(tr.at[3], ysend.at[3])
-    send_row(lambda r: ysend.at[3, r], yr.at[3], Y4, block)
-    yr[3, block] = ysend[3, row]
-    wait_all(zr.at[2], Z3, col)
+    send_row(lambda r: ysend.at[3, r], yr.at[3], Y4, block, ysend.at[3, pl.ds(0, N - 1)])
+    wait_recv(zr.at[2], Z3)
     out_z = pltpu.make_async_copy(zr.at[2], zsum, loc_sem.at[2])
     out_z.start()
     pending.append(out_z.wait)
-    wait_all(yr.at[3], Y4, block)
+    wait_recv(yr.at[3], Y4)
     inverse_x(yr.at[3], xsend.at[1], xr.at[3], X4)
     def finish_block(m):
         at = pl.ds(4 * m, 4)
         gin_v[at] = (xr[3, m].astype(F32) + gz_v[at]).astype(BF)
 
     finish_block(col)
-    for x, y, c in COL_ORDER:
+
+    @pl.loop(0, N - 1)
+    def _(k):
+        x, y, c = ordered(k)
         m = col_partner(x, 4 - y, c, col_c ^ c)
         wait_recv(xr.at[3, m], X4, m)
         finish_block(m)
@@ -516,22 +503,33 @@
     finish()
 
 
-def last_kernel(gin, ug, zsum, gin_out, sg, pg, bg):
-    step = pl.program_id(0)
-    gin_out[...] = gin[...]
-
-    @pl.when(step == 0)
-    def _():
-        pg[...] = zsum[:, 0:4, 0:64].reshape(C, C) * SCALE
-        bg[...] = zsum[0, 4:5, 0:64] * SCALE
-
-    channel = (lax.broadcasted_iota(jnp.int32, (64, 1024), 1) >> 6) + 16 * step
-    own = lax.broadcasted_iota(jnp.int32, (64, 1024), 0)
-    ue = dot(ug[0].astype(BF), jnp.where(channel == own, 1.0, 0.0).astype(BF))
-    g = jnp.concatenate([ug[1]] * 16, 1)
-    ur, ui, gr, gi = ue[0:64], ue[64:128], g[0:64], g[64:128]
-    sg[0] = (gr * ur + gi * ui).reshape(8, 8, 1024)
-    sg[1] = (gi * ur - gr * ui).reshape(8, 8, 1024)
+def last_kernel(gin, ug, zsum, gin_out, sg, pg, bg, gin_v, ug_v, z_v, sg_v, sem):
+    pieces = ((ug, ug_v), (gin, gin_v), (zsum, z_v))
+    loads = [pltpu.make_async_copy(a, b, sem.at[i]) for i, (a, b) in enumerate(pieces)]
+    for load in loads:
+        load.start()
+    loads[0].wait()
+    u = ug_v[0].astype(BF)
+    g = jnp.concatenate([ug_v[1]] * 8, 1)
+    gr, gi = g[0:64], g[64:128]
+    own = lax.broadcasted_iota(jnp.int32, (64, 512), 0)
+    group = lax.broadcasted_iota(jnp.int32, (64, 512), 1) >> 6
+    out = pltpu.make_async_copy(gin_v, gin_out, sem.at[1])
+    for i in range(8):
+        at = slice(512 * i, 512 * i + 512)
+        ue = dot(u, jnp.where(group + 8 * i == own, 1.0, 0.0).astype(BF))
+        ur, ui = ue[0:64], ue[64:128]
+        sg_v[0, :, :, at] = (gr * ur + gi * ui).reshape(8, 8, 512)
+        sg_v[1, :, :, at] = (gi * ur - gr * ui).reshape(8, 8, 512)
+        pltpu.make_async_copy(sg_v.at[:, :, :, at], sg.at[:, :, :, at], sem.at[3]).start()
+        if i == 0:
+            loads[1].wait()
+            out.start()
+    loads[2].wait()
+    pg[...] = z_v[:, 0:4, 0:64].reshape(C, C) * SCALE
+    bg[...] = z_v[0, 4:5, 0:64] * SCALE
+    pltpu.make_async_copy(sg_v, sg, sem.at[3]).wait()
+    out.wait()
 
 
 def body(inputs, cotangent, spectral_weight, point_weight, bias):
@@ -574,7 +572,7 @@
             pltpu.VMEM((72, 1024), F32),
             pltpu.VMEM((2, 128, C), F32),
             pltpu.VMEM(field, BF),
-            pltpu.SemaphoreType.DMA((15, N)),
+            pltpu.SemaphoreType.DMA((15,)),
             pltpu.SemaphoreType.DMA((15, N)),
             pltpu.SemaphoreType.DMA((10,)),
         ],
@@ -582,24 +580,26 @@
             collective_id=0, has_side_effects=True, vmem_limit_bytes=VMEM_BYTES
         ),
     )(inputs, cotangent, spectral_weight, point_weight, bias, table)
-    channels = pl.BlockSpec((C // 4, TY, TX), lambda i: (i, 0, 0))
     whole = lambda shape: pl.BlockSpec(shape, lambda i: (0,) * len(shape))
     grad_input, spectral_grad, pointwise_grad, bias_grad = pl.pallas_call(
         last_kernel,
-        grid=(4,),
+        grid=(1,),
         out_shape=(
             jax.ShapeDtypeStruct(field, BF),
             jax.ShapeDtypeStruct((2, 8, 8, C * C), F32),
             jax.ShapeDtypeStruct((C, C), F32),
             jax.ShapeDtypeStruct((1, C), F32),
         ),
-        in_specs=[channels, whole((2, 128, C)), whole((N, 8, 128))],
-        out_specs=(
-            channels,
-            pl.BlockSpec((2, 8, 8, 1024), lambda i: (0, 0, 0, i)),
-            whole((C, C)),
-            whole((1, C)),
-        ),
+        in_specs=[any_spec] * 3,
+        out_specs=(any_spec, any_spec, whole((C, C)), whole((1, C))),
+        scratch_shapes=[
+            pltpu.VMEM(field, BF),
+            pltpu.VMEM((2, 128, C), F32),
+            pltpu.VMEM((N, 8, 128), F32),
+            pltpu.VMEM((2, 8, 8, C * C), F32),
+            pltpu.SemaphoreType.DMA((4,)),
+        ],
+        compiler_params=pltpu.CompilerParams(vmem_limit_bytes=VMEM_BYTES),
     )(grad_input, modes, sums)
     return grad_input, spectral_grad, pointwise_grad, bias_grad.reshape(C)
 

time: 138 us -> 131 us (0.949)
  Pallas kernels: 137 us -> 130 us
    pallas_call x1, Pallas kernels: 133 us -> 127 us  [body(): pl.pallas_call(kernel, out_shape=(jax.ShapeDtypeStruct(field, BF), jax.Sh...]
where the time goes in v3:
time: 131 us
  Pallas kernels  130 us (99%)
    pallas_call x1, Pallas kernels, body(): pl.pallas_call(kernel, out_shape=(jax.ShapeDtypeStruct(field, BF), jax.Sh...  127 us
    pallas_call x1, Pallas kernels, body(): pl.pallas_call(last_kernel, grid=(1,), out_shape=(jax.ShapeDtypeStruct(fi...  3.52 us

profile of v3, /device:TPU:1, one launch (start us, length us, event | category | flops | bytes accessed | tf_op | source)
XLA Modules:
  0.0 130.7 jit_solution(16321345931396621510)
XLA Ops:
  0.6 126.6 %shard_map.93 = (bf16[64,64,128]{2,1,0:T(8,128)(2,1)}, f32[2,128,64]{2,1,0:T(8,128)}, f32[16,8,128]{2,1,0:T(8,128)}) custom-call(bf16[64,64,128]{2,1,0:T(8,128)(2,1)} %inp.1, bf16[64,64,128]{2,1,0:T(8,128)(2,1)} %cot.1, bf16[2,8,8,4096]{3,2,1,0:T(8,128)(2,1)} %w.1, bf16[64,64]{1,0:T(8,128)(2,1)} %pw_hbm.1, f32[64]{0:T(128)} %bias_hbm.1, ...), custom_call_target="tpu_custom_call" | custom-call | tf_op jit(solution)/shard_map/pallas_call | solution.py:539
  127.2 3.5 %shard_map.94 = (bf16[64,64,128]{2,1,0:T(8,128)(2,1)}, f32[2,8,8,4096]{3,2,1,0:T(8,128)}, f32[64,64]{1,0:T(8,128)}, f32[1,64]{1,0:T(1,128)}) custom-call(bf16[64,64,128]{2,1,0:T(8,128)(2,1)} %get-tuple-element.11.gin, f32[2,128,64]{2,1,0:T(8,128)} %get-tuple-element.12.ug, f32[16,8,128]{2,1,0:T(8,128)} %get-tuple-element.13.zsum), custom_call_target="tpu_custom_call" | custom-call | tf_op jit(solution)/shard_map/pallas_call | solution.py:584

commit v4 on v3

--- a/solution.py
+++ b/solution.py
@@ -100,8 +100,8 @@
     def wait_sent(like, phase):
         remote(like, like, phase, 0, (row, col)).wait_send()
 
-    def keep(src, dst, phase):
-        pltpu.make_async_copy(src, dst, recv_sem.at[phase, 0]).start()
+    def keep(src, dst, phase, half=0):
+        pltpu.make_async_copy(src, dst, recv_sem.at[phase, half]).start()
 
     pending = []
 
@@ -128,14 +128,14 @@
         code = (jnp.where(k < 8, words[0], words[1]) >> (4 * lax.rem(k, 8))) & 15
         return code >> 3, (code >> 1) & 3, code & 1
 
-    def send_block(src, dst, m, phase):
-        remote(src, dst.at[col], phase, col, (row, m)).start()
-
-    def send_row(src_of, dst, phase, slot, like):
+    def send_block(src, dst, m, phase, half):
+        remote(src, dst.at[half, col], phase, N * half + col, (row, m)).start()
+
+    def send_row(src_of, dst, phase, slot, like, half=0):
         for x, z in ROW_ORDER:
             r = row_partner(x, z)
-            remote(src_of(r), dst.at[slot], phase, 0, (r, col)).start()
-        keep(src_of(row), dst.at[slot], phase)
+            remote(src_of(r), dst.at[slot], phase, half, (r, col)).start()
+        keep(src_of(row), dst.at[slot], phase, half)
         sent(like, phase)
 
     def send_col(src_of, dst, phase, like):
@@ -191,7 +191,8 @@
                 (bias_hbm, bias),
                 (inp, inp_v),
                 (tab, tab_v),
-                (inp.at[pl.ds(4 * col, 4)], xr.at[0, col]),
+                (inp.at[pl.ds(4 * col, 2)], xr.at[0, 0, col]),
+                (inp.at[pl.ds(4 * col + 2, 2)], xr.at[0, 1, col]),
                 (w, w_v),
                 (cot, cot_v),
             ]
@@ -201,9 +202,10 @@
         load.start()
     pl.semaphore_wait(barrier, 2 * N - 2)
 
-    for x, y, c in COL_ORDER:
-        m = col_partner(x, y, c, col_c)
-        send_block(inp.at[pl.ds(4 * m, 4)], xr.at[0], m, X1)
+    for half in range(2):
+        for x, y, c in COL_ORDER:
+            m = col_partner(x, y, c, col_c)
+            send_block(inp.at[pl.ds(4 * m + 2 * half, 2)], xr.at[0], m, X1, half)
     sent(inp.at[pl.ds(0, 4 * N - 4)], X1)
 
     def pack(src, dst):
@@ -233,8 +235,8 @@
                     y = 32 * h + 16 * t
                     dst[out, y : y + 16, :] = res[:, 128 * t : 128 * t + 128].reshape(16, 16, 128)
 
-    def forward_x(src, phase, dst):
-        acc = jnp.zeros((256, 256), F32)
+    def forward_x(src, phase, dst, half):
+        acc = jnp.zeros((256, 128), F32)
         for x, y in CHIPS:
             chip = 4 * (col_x ^ x) + lax.rem(col_y + y, 4)
             blocks = []
@@ -243,32 +245,30 @@
 
                 @pl.when(slot != col)
                 def _(slot=slot):
-                    wait_recv(src.at[slot], phase, slot)
-
-                blocks.append(src[slot].reshape(256, 128))
+                    wait_recv(src.at[half, slot], phase, N * half + slot)
+
+                blocks.append(src[half, slot].reshape(128, 128))
             acc = acc + dot_t(tab_v[chip], jnp.concatenate(blocks, 1))
-        dst[...] = acc.astype(BF).reshape(N, 16, 256)
-
-    def forward_y(src, dst):
-        acc = jnp.zeros((K1, 64), F32)
-        for q in range(4):
+        dst[...] = acc.astype(BF).reshape(N, 16, 128)
+
+    def forward_y(src):
+        acc = jnp.zeros((K1, 32), F32)
+        for q in range(8):
             parts = []
-            for t in range(4):
-                b = src[4 * q + t].astype(F32)
+            for t in range(2):
+                b = src[2 * q + t].astype(F32)
                 jb = jnp.concatenate([b[8:16], -b[0:8]], 0)
-                rows = []
-                for h in range(2):
-                    bh = b[:, 128 * h : 128 * h + 128]
-                    jh = jb[:, 128 * h : 128 * h + 128]
-                    rows.append(jnp.where(lane_lo, bh, pltpu.roll(jh, 64, 1)))
-                    rows.append(jnp.where(lane_lo, pltpu.roll(bh, 64, 1), jh))
+                rows = [
+                    jnp.where(lane_lo, b, pltpu.roll(jb, 64, 1)),
+                    jnp.where(lane_lo, pltpu.roll(b, 64, 1), jb),
+                ]
                 parts.append(jnp.concatenate(rows, 0).astype(BF))
-            for h in range(2):
-                table = tab_v[8 + q, 128 * h : 128 * h + 128, :]
-                acc = acc + dot_t(table, jnp.concatenate(parts[2 * h : 2 * h + 2], 1))
-        res = (acc * SCALE).astype(BF).astype(F32)
-        res = res.reshape(N, 8, 64)
-        dst[...] = jnp.concatenate([res[:, 0:4], res[:, 4:8]], 2)
+            table = tab_v[8 + q // 2, 128 * (q % 2) : 128 * (q % 2) + 128, :]
+            acc = acc + dot_t(table, jnp.concatenate(parts, 1))
+        return (acc * SCALE).astype(BF).astype(F32).reshape(N, 8, 32)
+
+    def pack_t(first, second, dst):
+        dst[...] = jnp.concatenate([first[:, 0:4], second[:, 0:4], first[:, 4:8], second[:, 4:8]], 2)
 
     def unpack_t(src):
         x = src[...]
@@ -298,7 +298,7 @@
         x = xt.T.reshape(N, 8, 128)
         dst[...] = jnp.concatenate([x[:, 0:4, 0:64], x[:, 4:8, 0:64]], 2)
 
-    def inverse_y(src, dst):
+    def inverse_y(src):
         ht = unpack_t(src)
         first, second = [], []
         for c in range(4):
@@ -306,34 +306,34 @@
             first += [hr, hi]
             second += [-hi, hr]
         h = jnp.concatenate([jnp.concatenate(first, 0), jnp.concatenate(second, 0)], 1).astype(BF)
+        return h
+
+    def inverse_y_half(h, dst, half):
+        h = h[32 * half : 32 * half + 32]
         d = jnp.concatenate([dot(h, tab_v[12 + i]) for i in range(4)], 1)
         for a in range(8):
-            for p in range(2):
-                t0 = d[32 * p : 32 * p + 16, 128 * a : 128 * a + 128]
-                t1 = d[32 * p + 16 : 32 * p + 32, 128 * a : 128 * a + 128]
-                at = slice(128 * p, 128 * p + 128)
-                dst[2 * a, :, at] = jnp.where(lane_lo, t0, pltpu.roll(t1, 64, 1)).astype(BF)
-                dst[2 * a + 1, :, at] = jnp.where(lane_lo, pltpu.roll(t0, 64, 1), t1).astype(BF)
-
-    def inverse_x(src, out, dst, phase):
-        yt = src[...].reshape(256, 256).astype(F32).T.astype(BF)
+            t0 = d[0:16, 128 * a : 128 * a + 128]
+            t1 = d[16:32, 128 * a : 128 * a + 128]
+            dst[2 * a] = jnp.where(lane_lo, t0, pltpu.roll(t1, 64, 1)).astype(BF)
+            dst[2 * a + 1] = jnp.where(lane_lo, pltpu.roll(t0, 64, 1), t1).astype(BF)
+
+    def inverse_x(src, out, dst, phase, half):
+        yt = src[...].reshape(256, 128).astype(F32).T.astype(BF)
         late = None
         for x, y in CHIPS:
             chip = 4 * (col_x ^ x) + lax.rem(col_y + jnp.where(col_c == 0, y, 4 - y), 4)
             res = (dot(yt, tab_v[chip]) * SCALE).astype(BF)
             for c in range(2):
-                out[2 * chip + c] = res[:, 128 * c : 128 * c + 128].reshape(4, TY, TX)
+                out[half, 2 * chip + c] = res[:, 128 * c : 128 * c + 128].reshape(2, TY, TX)
             m = 2 * chip + col_c
             if (x, y) != (0, 0):
-                send_block(out.at[m], dst, m, phase)
+                send_block(out.at[half, m], dst, m, phase, half)
             else:
-                dst[m] = out[m]
+                dst[half, m] = out[half, m]
             if late is not None:
-                send_block(out.at[late], dst, late, phase)
+                send_block(out.at[half, late], dst, late, phase, half)
             late = m ^ 1
-        send_block(out.at[late], dst, late, phase)
-
-        sent(out.at[pl.ds(0, N - 1)], phase)
+        send_block(out.at[half, late], dst, late, phase, half)
 
     lane = lax.broadcasted_iota(jnp.int32, (1024, 64), 1)
     first = lax.broadcasted_iota(jnp.int32, (1024, 64), 0)
@@ -357,13 +357,24 @@
 
     loads[3].wait()
     loads[4].wait()
-    forward_x(xr.at[0], X1, ysend.at[0])
-    send_row(lambda r: ysend.at[0, wrap(r + col)], yr.at[0], Y1, row, ysend.at[0, pl.ds(0, N - 1)])
+    loads[5].wait()
+    for half in range(2):
+        forward_x(xr.at[0], X1, ysend.at[0, half], half)
+        send_row(
+            lambda r, half=half: ysend.at[0, half, wrap(r + col)],
+            yr.at[0, half],
+            Y1,
+            row,
+            ysend.at[0, half, pl.ds(0, N - 1)],
+            half,
+        )
     build_kron(1)
-    wait_recv(yr.at[0], Y1)
-    forward_y(yr.at[0], tsend.at[0])
+    wait_recv(yr.at[0, 0], Y1, 0)
+    first_half = forward_y(yr.at[0, 0])
+    wait_recv(yr.at[0, 1], Y1, 1)
+    pack_t(first_half, forward_y(yr.at[0, 1]), tsend.at[0])
     send_t(tsend.at[0], tr.at[0], T1, True)
-    loads[5].wait()
+    loads[6].wait()
     wait_recv(tr.at[0], T1)
 
     u = to_modes(tr.at[0])
@@ -383,36 +394,49 @@
         return sr + fold(wr * ur - wi * ui), si + fold(wr * ui + wi * ur)
 
     zero = jnp.zeros((64, 128), F32)
-    sr, si = lax.fori_loop(0, 8, mix, (zero, zero))
+    sr, si = lax.fori_loop(0, 8, mix, (zero, zero), unroll=True)
     both = jnp.concatenate([sr, si], 0)
     both = both + pltpu.roll(both, 64, 1)
     from_modes(both[:, 0:64], tsend.at[1])
     send_t(tsend.at[1], tr.at[1], T2, False)
 
     wait_recv(tr.at[1], T2)
-    inverse_y(tr.at[1], ysend.at[1])
-    send_row(lambda r: ysend.at[1, r], yr.at[1], Y2, block, ysend.at[1, pl.ds(0, N - 1)])
-    wait_recv(yr.at[1], Y2)
-    inverse_x(yr.at[1], xsend.at[0], xr.at[1], X2)
+    spec = inverse_y(tr.at[1])
+    for half in range(2):
+        inverse_y_half(spec, ysend.at[1, half], half)
+        send_row(
+            lambda r, half=half: ysend.at[1, half, r],
+            yr.at[1, half],
+            Y2,
+            block,
+            ysend.at[1, half, pl.ds(0, N - 1)],
+            half,
+        )
+    for half in range(2):
+        wait_recv(yr.at[1, half], Y2, half)
+        inverse_x(yr.at[1, half], xsend.at[0], xr.at[1], X2, half)
+        sent(xsend.at[0, half, pl.ds(0, N - 1)], X2)
 
     loads[1].wait()
-    loads[6].wait()
-    def slope(m):
-        for c in range(4):
-            z = xr[1, m, c].astype(F32) + zp_v[4 * m + c] + bias[4 * m + c]
-            dz = cot_v[4 * m + c].astype(F32) * normal_slope(z)
-            dz_v[4 * m + c] = dz.astype(BF)
-
-    slope(col)
-    xr[2, col] = dz_v[pl.ds(4 * col, 4)]
-
-    @pl.loop(0, N - 1)
-    def _(k):
-        x, y, c = ordered(k)
-        m = col_partner(x, 4 - y, c, col_c ^ c)
-        wait_recv(xr.at[1, m], X2, m)
-        slope(m)
-        send_block(dz_v.at[pl.ds(4 * m, 4)], xr.at[2], m, X3)
+    loads[7].wait()
+    def slope(m, half):
+        for c in range(2):
+            at = 4 * m + 2 * half + c
+            z = xr[1, half, m, c].astype(F32) + zp_v[at] + bias[at]
+            dz = cot_v[at].astype(F32) * normal_slope(z)
+            dz_v[at] = dz.astype(BF)
+
+    for half in range(2):
+        slope(col, half)
+        xr[2, half, col] = dz_v[pl.ds(4 * col + 2 * half, 2)]
+
+        @pl.loop(0, N - 1)
+        def _(k, half=half):
+            x, y, c = ordered(k)
+            m = col_partner(x, 4 - y, c, col_c ^ c)
+            wait_recv(xr.at[1, half, m], X2, N * half + m)
+            slope(m, half)
+            send_block(dz_v.at[pl.ds(4 * m + 2 * half, 2)], xr.at[2], m, X3, half)
 
     sent(dz_v.at[pl.ds(0, 4 * N - 4)], X3)
 
@@ -440,10 +464,20 @@
     send_col(lambda m: zsend.at[m], zr.at[0], Z1, zsend.at[pl.ds(0, N - 1)])
     apply_kron(1, dz2_v, gz_v)
 
-    forward_x(xr.at[2], X3, ysend.at[2])
-    send_row(lambda r: ysend.at[2, wrap(r + col)], yr.at[2], Y3, row, ysend.at[2, pl.ds(0, N - 1)])
-    wait_recv(yr.at[2], Y3)
-    forward_y(yr.at[2], tsend.at[2])
+    for half in range(2):
+        forward_x(xr.at[2], X3, ysend.at[2, half], half)
+        send_row(
+            lambda r, half=half: ysend.at[2, half, wrap(r + col)],
+            yr.at[2, half],
+            Y3,
+            row,
+            ysend.at[2, half, pl.ds(0, N - 1)],
+            half,
+        )
+    wait_recv(yr.at[2, 0], Y3, 0)
+    first_half = forward_y(yr.at[2, 0])
+    wait_recv(yr.at[2, 1], Y3, 1)
+    pack_t(first_half, forward_y(yr.at[2, 1]), tsend.at[2])
     send_t(tsend.at[2], tr.at[2], T3, True)
     wait_recv(zr.at[0], Z1)
     zr[3, 0] = jnp.sum(zr[0], axis=0)
@@ -463,7 +497,7 @@
         both = jnp.concatenate([wr * gr4 + wi * gi4, wr * gi4 - wi * gr4], 0).astype(BF)
         return acc + dot_t(both, e_v[:, at])
 
-    du = lax.fori_loop(0, 8, mix_back, jnp.zeros((128, 64), F32))
+    du = lax.fori_loop(0, 8, mix_back, jnp.zeros((128, 64), F32), unroll=True)
     from_modes(du, tsend.at[3])
     send_t(tsend.at[3], tr.at[3], T4, False)
 
@@ -474,26 +508,38 @@
     out_ug.start()
 
     wait_recv(tr.at[3], T4)
-    inverse_y(tr.at[3], ysend.at[3])
-    send_row(lambda r: ysend.at[3, r], yr.at[3], Y4, block, ysend.at[3, pl.ds(0, N - 1)])
+    spec = inverse_y(tr.at[3])
+    for half in range(2):
+        inverse_y_half(spec, ysend.at[3, half], half)
+        send_row(
+            lambda r, half=half: ysend.at[3, half, r],
+            yr.at[3, half],
+            Y4,
+            block,
+            ysend.at[3, half, pl.ds(0, N - 1)],
+            half,
+        )
     wait_recv(zr.at[2], Z3)
     out_z = pltpu.make_async_copy(zr.at[2], zsum, loc_sem.at[2])
     out_z.start()
     pending.append(out_z.wait)
-    wait_recv(yr.at[3], Y4)
-    inverse_x(yr.at[3], xsend.at[1], xr.at[3], X4)
-    def finish_block(m):
-        at = pl.ds(4 * m, 4)
-        gin_v[at] = (xr[3, m].astype(F32) + gz_v[at]).astype(BF)
-
-    finish_block(col)
-
-    @pl.loop(0, N - 1)
-    def _(k):
-        x, y, c = ordered(k)
-        m = col_partner(x, 4 - y, c, col_c ^ c)
-        wait_recv(xr.at[3, m], X4, m)
-        finish_block(m)
+    for half in range(2):
+        wait_recv(yr.at[3, half], Y4, half)
+        inverse_x(yr.at[3, half], xsend.at[1], xr.at[3], X4, half)
+        sent(xsend.at[1, half, pl.ds(0, N - 1)], X4)
+    def finish_block(m, half):
+        at = pl.ds(4 * m + 2 * half, 2)
+        gin_v[at] = (xr[3, half, m].astype(F32) + gz_v[at]).astype(BF)
+
+    for half in range(2):
+        finish_block(col, half)
+
+        @pl.loop(0, N - 1)
+        def _(k, half=half):
+            x, y, c = ordered(k)
+            m = col_partner(x, 4 - y, c, col_c ^ c)
+            wait_recv(xr.at[3, half, m], X4, N * half + m)
+            finish_block(m, half)
 
     out_gin = pltpu.make_async_copy(gin_v, gin, loc_sem.at[1])
     out_gin.start()
@@ -555,11 +601,11 @@
             pltpu.VMEM((512, 64), BF),
             pltpu.VMEM((64, C * C), BF),
             pltpu.VMEM((1024, 64), BF),
-            pltpu.VMEM((4, N, 4, TY, TX), BF),
-            pltpu.VMEM((4, N, 16, 256), BF),
+            pltpu.VMEM((4, 2, N, 2, TY, TX), BF),
+            pltpu.VMEM((4, 2, N, 16, 128), BF),
             pltpu.VMEM((4, N, 4, 128), F32),
-            pltpu.VMEM((2, N, 4, TY, TX), BF),
-            pltpu.VMEM((4, N, 16, 256), BF),
+            pltpu.VMEM((2, 2, N, 2, TY, TX), BF),
+            pltpu.VMEM((4, 2, N, 16, 128), BF),
             pltpu.VMEM((4, N, 4, 128), F32),
             pltpu.VMEM((N, 8, 128), F32),
             pltpu.VMEM((4, N, 8, 128), F32),
@@ -573,7 +619,7 @@
             pltpu.VMEM((2, 128, C), F32),
             pltpu.VMEM(field, BF),
             pltpu.SemaphoreType.DMA((15,)),
-            pltpu.SemaphoreType.DMA((15, N)),
+            pltpu.SemaphoreType.DMA((15, 2 * N)),
             pltpu.SemaphoreType.DMA((10,)),
         ],
         compiler_params=pltpu.CompilerParams(

time: 131 us -> 129 us (0.985)
  Pallas kernels: 130 us -> 128 us
    pallas_call x1, Pallas kernels: 127 us -> 125 us  [body(): pl.pallas_call(kernel, out_shape=(jax.ShapeDtypeStruct(field, BF), jax.Sh...]
where the time goes in v4:
time: 129 us
  Pallas kernels  128 us (99%)
    pallas_call x1, Pallas kernels, body(): pl.pallas_call(kernel, out_shape=(jax.ShapeDtypeStruct(field, BF), jax.Sh...  125 us
    pallas_call x1, Pallas kernels, body(): pl.pallas_call(last_kernel, grid=(1,), out_shape=(jax.ShapeDtypeStruct(fi...  3.52 us

profile of v4, /device:TPU:1, one launch (start us, length us, event | category | flops | bytes accessed | tf_op | source)
XLA Modules:
  0.0 129.1 jit_solution(13976453600233019585)
XLA Ops:
  0.6 124.9 %shard_map.93 = (bf16[64,64,128]{2,1,0:T(8,128)(2,1)}, f32[2,128,64]{2,1,0:T(8,128)}, f32[16,8,128]{2,1,0:T(8,128)}) custom-call(bf16[64,64,128]{2,1,0:T(8,128)(2,1)} %inp.1, bf16[64,64,128]{2,1,0:T(8,128)(2,1)} %cot.1, bf16[2,8,8,4096]{3,2,1,0:T(8,128)(2,1)} %w.1, bf16[64,64]{1,0:T(8,128)(2,1)} %pw_hbm.1, f32[64]{0:T(128)} %bias_hbm.1, ...), custom_call_target="tpu_custom_call" | custom-call | tf_op jit(solution)/shard_map/pallas_call | solution.py:585
  125.6 3.5 %shard_map.94 = (bf16[64,64,128]{2,1,0:T(8,128)(2,1)}, f32[2,8,8,4096]{3,2,1,0:T(8,128)}, f32[64,64]{1,0:T(8,128)}, f32[1,64]{1,0:T(1,128)}) custom-call(bf16[64,64,128]{2,1,0:T(8,128)(2,1)} %get-tuple-element.11.gin, f32[2,128,64]{2,1,0:T(8,128)} %get-tuple-element.12.ug, f32[16,8,128]{2,1,0:T(8,128)} %get-tuple-element.13.zsum), custom_call_target="tpu_custom_call" | custom-call | tf_op jit(solution)/shard_map/pallas_call | solution.py:630

commit v5 on v4

--- a/solution.py
+++ b/solution.py
@@ -47,8 +47,11 @@
     cos, sin = trig(np.arange(K1) - K1 // 2, np.arange(NY), NY)
     ty = np.stack([cos.reshape(K1, N, TY), sin.reshape(K1, N, TY)], 2).reshape(K1, 8, 256)
     ty = ty.transpose(1, 0, 2).reshape(4, 256, 256)
-    tyi = np.concatenate([cos, sin], 0).reshape(2 * K1, 4, 256).transpose(1, 0, 2)
-    return np.ascontiguousarray(np.concatenate([tx, ty, tyi], 0))
+    c4, s4 = (t.reshape(N, 8, N, TY).transpose(2, 3, 0, 1) for t in (cos, sin))
+    back = np.stack([np.stack([c4, -s4], 3), np.stack([s4, c4], 3)], 1).reshape(N, 2 * TY, 2 * K1)
+    cos, sin = trig(np.arange(K2), np.arange(NX), NX)
+    txb = np.concatenate([cos, -sin], 0).reshape(2 * K2, 8, NX // 8).transpose(1, 0, 2)
+    return np.ascontiguousarray(np.concatenate([tx, ty, txb], 0)), np.ascontiguousarray(back)
 
 
 def dot(a, b):
@@ -66,10 +69,10 @@
 
 
 def kernel(
-    inp, cot, w, pw_hbm, bias_hbm, tab,
+    inp, cot, w, pw_hbm, bias_hbm, tab, back,
     gin, ug, zsum,
-    pw, bias, inp_v, cot_v, w_v, tab_v, e1_v, e_v, sel_v,
-    xr, yr, tr, xsend, ysend, tsend,
+    pw, bias, inp_v, cot_v, w_v, tab_v, back_v, e1_v, e_v, sel_v,
+    xr, yr, tr, xsend, ysend, tsend, gsend, gath,
     zsend, zr, f2_v, dz_v, dz2_v, kron_v, zp_v, gz_v, s_v, ug_v, gin_v,
     send_sem, recv_sem, loc_sem,
 ):
@@ -81,6 +84,10 @@
         jnp.int32, (8, 8, 128), 0
     )
 
+    mask_k = (lax.broadcasted_iota(jnp.int32, (8, 8, 128), 2) & 7) == lax.broadcasted_iota(
+        jnp.int32, (8, 8, 128), 1
+    )
+
     def wrap(i):
         return lax.rem(i, N)
 
@@ -148,22 +155,18 @@
     block = wrap(row + col)
     top = row == 0
 
-    def send_t(src, dst, phase, to_modes):
-        own = row if to_modes else col
-        slot = col if to_modes else row
-
+    def send_t(src, dst, phase):
         @pl.loop(0, N)
         def _(i):
-            target = (i, block) if to_modes else (wrap(col + N - i), i)
-            is_own = jnp.logical_and(top, i == own)
+            is_own = jnp.logical_and(top, i == row)
 
             @pl.when(jnp.logical_not(is_own))
             def _():
-                remote(src.at[i], dst.at[slot], phase, 0, target).start()
+                remote(src.at[i], dst.at[col], phase, 0, (i, block)).start()
 
             @pl.when(is_own)
             def _():
-                keep(src.at[i], dst.at[slot], phase)
+                keep(src.at[i], dst.at[col], phase)
 
         def wait():
             @pl.when(top)
@@ -195,6 +198,7 @@
                 (inp.at[pl.ds(4 * col + 2, 2)], xr.at[0, 1, col]),
                 (w, w_v),
                 (cot, cot_v),
+                (back.at[row], back_v),
             ]
         )
     ]
@@ -293,36 +297,26 @@
         for c in range(4):
             for ri in range(2):
                 part = full[64 * ri : 64 * ri + 64, 128 * c : 128 * c + 128].reshape(8, 8, 128)
-                tiles.append(jnp.sum(jnp.where(mask_j, part, 0.0), axis=0))
+                tiles.append(jnp.sum(jnp.where(mask_k, part, 0.0), axis=1))
         xt = jnp.concatenate(tiles + [jnp.zeros((64, 128), F32)], 0)
         x = xt.T.reshape(N, 8, 128)
         dst[...] = jnp.concatenate([x[:, 0:4, 0:64], x[:, 4:8, 0:64]], 2)
 
-    def inverse_y(src):
-        ht = unpack_t(src)
-        first, second = [], []
-        for c in range(4):
-            hr, hi = ht[16 * c : 16 * c + 8], ht[16 * c + 8 : 16 * c + 16]
-            first += [hr, hi]
-            second += [-hi, hr]
-        h = jnp.concatenate([jnp.concatenate(first, 0), jnp.concatenate(second, 0)], 1).astype(BF)
-        return h
-
-    def inverse_y_half(h, dst, half):
-        h = h[32 * half : 32 * half + 32]
-        d = jnp.concatenate([dot(h, tab_v[12 + i]) for i in range(4)], 1)
-        for a in range(8):
-            t0 = d[0:16, 128 * a : 128 * a + 128]
-            t1 = d[16:32, 128 * a : 128 * a + 128]
-            dst[2 * a] = jnp.where(lane_lo, t0, pltpu.roll(t1, 64, 1)).astype(BF)
-            dst[2 * a + 1] = jnp.where(lane_lo, pltpu.roll(t0, 64, 1), t1).astype(BF)
+    def spread_modes(src, dst):
+        xt = unpack_t(src)
+        for half in range(2):
+            pair = [xt[32 * half + 16 * c : 32 * half + 16 * c + 16] for c in range(2)]
+            dst[half] = jnp.concatenate(pair, 1).astype(BF)
 
     def inverse_x(src, out, dst, phase, half):
-        yt = src[...].reshape(256, 128).astype(F32).T.astype(BF)
+        d = dot(back_v[...], src[...].reshape(256, 256)).astype(BF)
+        real, imag = d[0:TY], d[TY : 2 * TY]
+        rows = [jnp.concatenate([real[:, at : at + 128], imag[:, at : at + 128]], 1) for at in (0, 128)]
+        yt = jnp.concatenate(rows, 0)
         late = None
         for x, y in CHIPS:
             chip = 4 * (col_x ^ x) + lax.rem(col_y + jnp.where(col_c == 0, y, 4 - y), 4)
-            res = (dot(yt, tab_v[chip]) * SCALE).astype(BF)
+            res = (dot(yt, tab_v[12 + chip]) * SCALE).astype(BF)
             for c in range(2):
                 out[half, 2 * chip + c] = res[:, 128 * c : 128 * c + 128].reshape(2, TY, TX)
             m = 2 * chip + col_c
@@ -373,8 +367,9 @@
     first_half = forward_y(yr.at[0, 0])
     wait_recv(yr.at[0, 1], Y1, 1)
     pack_t(first_half, forward_y(yr.at[0, 1]), tsend.at[0])
-    send_t(tsend.at[0], tr.at[0], T1, True)
+    send_t(tsend.at[0], tr.at[0], T1)
     loads[6].wait()
+    loads[8].wait()
     wait_recv(tr.at[0], T1)
 
     u = to_modes(tr.at[0])
@@ -398,23 +393,22 @@
     both = jnp.concatenate([sr, si], 0)
     both = both + pltpu.roll(both, 64, 1)
     from_modes(both[:, 0:64], tsend.at[1])
-    send_t(tsend.at[1], tr.at[1], T2, False)
+    send_col(lambda m: tsend.at[1, m], tr.at[1], T2, tsend.at[1, pl.ds(0, N - 1)])
 
     wait_recv(tr.at[1], T2)
-    spec = inverse_y(tr.at[1])
-    for half in range(2):
-        inverse_y_half(spec, ysend.at[1, half], half)
+    spread_modes(tr.at[1], gsend.at[0])
+    for half in range(2):
         send_row(
-            lambda r, half=half: ysend.at[1, half, r],
-            yr.at[1, half],
+            lambda r, half=half: gsend.at[0, half],
+            gath.at[0, half],
             Y2,
-            block,
-            ysend.at[1, half, pl.ds(0, N - 1)],
+            row,
+            gath.at[0, half, pl.ds(0, N - 1)],
             half,
         )
     for half in range(2):
-        wait_recv(yr.at[1, half], Y2, half)
-        inverse_x(yr.at[1, half], xsend.at[0], xr.at[1], X2, half)
+        wait_recv(gath.at[0, half], Y2, half)
+        inverse_x(gath.at[0, half], xsend.at[0], xr.at[1], X2, half)
         sent(xsend.at[0, half, pl.ds(0, N - 1)], X2)
 
     loads[1].wait()
@@ -478,7 +472,7 @@
     first_half = forward_y(yr.at[2, 0])
     wait_recv(yr.at[2, 1], Y3, 1)
     pack_t(first_half, forward_y(yr.at[2, 1]), tsend.at[2])
-    send_t(tsend.at[2], tr.at[2], T3, True)
+    send_t(tsend.at[2], tr.at[2], T3)
     wait_recv(zr.at[0], Z1)
     zr[3, 0] = jnp.sum(zr[0], axis=0)
     send_row(lambda r: zr.at[3, 0], zr.at[1], Z2, row, zsend.at[pl.ds(0, N - 1)])
@@ -499,24 +493,24 @@
 
     du = lax.fori_loop(0, 8, mix_back, jnp.zeros((128, 64), F32), unroll=True)
     from_modes(du, tsend.at[3])
-    send_t(tsend.at[3], tr.at[3], T4, False)
+    send_col(lambda m: tsend.at[3, m], tr.at[3], T4, tsend.at[3, pl.ds(0, N - 1)])
 
     wait_recv(zr.at[1], Z2)
     zr[3, 1] = jnp.sum(zr[1], axis=0)
     send_col(lambda m: zr.at[3, 1], zr.at[2], Z3, zsend.at[pl.ds(0, N - 1)])
     out_ug = pltpu.make_async_copy(ug_v, ug, loc_sem.at[0])
     out_ug.start()
+    pending.append(out_ug.wait)
 
     wait_recv(tr.at[3], T4)
-    spec = inverse_y(tr.at[3])
-    for half in range(2):
-        inverse_y_half(spec, ysend.at[3, half], half)
+    spread_modes(tr.at[3], gsend.at[1])
+    for half in range(2):
         send_row(
-            lambda r, half=half: ysend.at[3, half, r],
-            yr.at[3, half],
+            lambda r, half=half: gsend.at[1, half],
+            gath.at[1, half],
             Y4,
-            block,
-            ysend.at[3, half, pl.ds(0, N - 1)],
+            row,
+            gath.at[1, half, pl.ds(0, N - 1)],
             half,
         )
     wait_recv(zr.at[2], Z3)
@@ -524,12 +518,14 @@
     out_z.start()
     pending.append(out_z.wait)
     for half in range(2):
-        wait_recv(yr.at[3, half], Y4, half)
-        inverse_x(yr.at[3, half], xsend.at[1], xr.at[3], X4, half)
-        sent(xsend.at[1, half, pl.ds(0, N - 1)], X4)
+        wait_recv(gath.at[1, half], Y4, half)
+        inverse_x(gath.at[1, half], xsend.at[1], xr.at[3], X4, half)
+    finish()
+
     def finish_block(m, half):
         at = pl.ds(4 * m + 2 * half, 2)
         gin_v[at] = (xr[3, half, m].astype(F32) + gz_v[at]).astype(BF)
+        pltpu.make_async_copy(gin_v.at[at], gin.at[at], loc_sem.at[1]).start()
 
     for half in range(2):
         finish_block(col, half)
@@ -541,15 +537,14 @@
             wait_recv(xr.at[3, half, m], X4, N * half + m)
             finish_block(m, half)
 
-    out_gin = pltpu.make_async_copy(gin_v, gin, loc_sem.at[1])
-    out_gin.start()
-
-    pending.append(out_ug.wait)
-    pending.append(out_gin.wait)
-    finish()
-
-
-def last_kernel(gin, ug, zsum, gin_out, sg, pg, bg, gin_v, ug_v, z_v, sg_v, sem):
+    wait_sent(xsend.at[1, 0, pl.ds(0, N - 1)], X4)
+    wait_sent(xsend.at[1, 1, pl.ds(0, N - 1)], X4)
+    pltpu.make_async_copy(gin_v, gin, loc_sem.at[1]).wait()
+
+
+def last_kernel(
+    gin, ug, zsum, gin_out, sg, pg, bg, gin_v, ug_v, z_v, sg_v, pg_v, bg_v, sem
+):
     pieces = ((ug, ug_v), (gin, gin_v), (zsum, z_v))
     loads = [pltpu.make_async_copy(a, b, sem.at[i]) for i, (a, b) in enumerate(pieces)]
     for load in loads:
@@ -571,17 +566,25 @@
         if i == 0:
             loads[1].wait()
             out.start()
-    loads[2].wait()
-    pg[...] = z_v[:, 0:4, 0:64].reshape(C, C) * SCALE
-    bg[...] = z_v[0, 4:5, 0:64] * SCALE
+            loads[2].wait()
+            pg_v[...] = z_v[:, 0:4, 0:64].reshape(C, C) * SCALE
+            bg_v[...] = z_v[0, 4:5, 0:64] * SCALE
+            sums = (
+                pltpu.make_async_copy(pg_v, pg, sem.at[0]),
+                pltpu.make_async_copy(bg_v, bg, sem.at[2]),
+            )
+            for copy in sums:
+                copy.start()
+    for copy in sums:
+        copy.wait()
+    out.wait()
     pltpu.make_async_copy(sg_v, sg, sem.at[3]).wait()
-    out.wait()
 
 
 def body(inputs, cotangent, spectral_weight, point_weight, bias):
     any_spec = pl.BlockSpec(memory_space=pl.ANY)
     field = (C, TY, TX)
-    table = jnp.asarray(tables())
+    table, back = (jnp.asarray(t) for t in tables())
     grad_input, modes, sums = pl.pallas_call(
         kernel,
         out_shape=(
@@ -589,7 +592,7 @@
             jax.ShapeDtypeStruct((2, 128, C), F32),
             jax.ShapeDtypeStruct((N, 8, 128), F32),
         ),
-        in_specs=[any_spec] * 6,
+        in_specs=[any_spec] * 7,
         out_specs=(any_spec, any_spec, any_spec),
         scratch_shapes=[
             pltpu.VMEM((C, C), BF),
@@ -598,6 +601,7 @@
             pltpu.VMEM(field, BF),
             pltpu.VMEM((2, 8, 8, C * C), BF),
             pltpu.VMEM(table.shape, BF),
+            pltpu.VMEM(back.shape[1:], BF),
             pltpu.VMEM((512, 64), BF),
             pltpu.VMEM((64, C * C), BF),
             pltpu.VMEM((1024, 64), BF),
@@ -607,6 +611,8 @@
             pltpu.VMEM((2, 2, N, 2, TY, TX), BF),
             pltpu.VMEM((4, 2, N, 16, 128), BF),
             pltpu.VMEM((4, N, 4, 128), F32),
+            pltpu.VMEM((2, 2, 16, 256), BF),
+            pltpu.VMEM((2, 2, N, 16, 256), BF),
             pltpu.VMEM((N, 8, 128), F32),
             pltpu.VMEM((4, N, 8, 128), F32),
             pltpu.VMEM((1024, 512), BF),
@@ -625,11 +631,9 @@
         compiler_params=pltpu.CompilerParams(
             collective_id=0, has_side_effects=True, vmem_limit_bytes=VMEM_BYTES
         ),
-    )(inputs, cotangent, spectral_weight, point_weight, bias, table)
-    whole = lambda shape: pl.BlockSpec(shape, lambda i: (0,) * len(shape))
+    )(inputs, cotangent, spectral_weight, point_weight, bias, table, back)
     grad_input, spectral_grad, pointwise_grad, bias_grad = pl.pallas_call(
         last_kernel,
-        grid=(1,),
         out_shape=(
             jax.ShapeDtypeStruct(field, BF),
             jax.ShapeDtypeStruct((2, 8, 8, C * C), F32),
@@ -637,12 +641,14 @@
             jax.ShapeDtypeStruct((1, C), F32),
         ),
         in_specs=[any_spec] * 3,
-        out_specs=(any_spec, any_spec, whole((C, C)), whole((1, C))),
+        out_specs=(any_spec,) * 4,
         scratch_shapes=[
             pltpu.VMEM(field, BF),
             pltpu.VMEM((2, 128, C), F32),
             pltpu.VMEM((N, 8, 128), F32),
             pltpu.VMEM((2, 8, 8, C * C), F32),
+            pltpu.VMEM((C, C), F32),
+            pltpu.VMEM((1, C), F32),
             pltpu.SemaphoreType.DMA((4,)),
         ],
         compiler_params=pltpu.CompilerParams(vmem_limit_bytes=VMEM_BYTES),

time: 129 us -> 127 us (0.984)
  Pallas kernels: 128 us -> 126 us
    pallas_call x1, Pallas kernels: 125 us -> 123 us  [body(): pl.pallas_call(kernel, out_shape=(jax.ShapeDtypeStruct(field, BF), jax.Sh...]
where the time goes in v5:
time: 127 us; the launch traced here: 126 us
  Pallas kernels  126 us (99%)
    pallas_call x1, Pallas kernels, body(): pl.pallas_call(kernel, out_shape=(jax.ShapeDtypeStruct(field, BF), jax.Sh...  123 us
    pallas_call x1, Pallas kernels, body(): pl.pallas_call(last_kernel, out_shape=(jax.ShapeDtypeStruct(field, BF), j...  2.91 us

profile of v5, /device:TPU:1, one launch (start us, length us, event | category | flops | bytes accessed | tf_op | source)
XLA Modules:
  0.0 126.5 jit_solution(778923380882345883)
XLA Ops:
  0.6 122.9 %shard_map.102 = (bf16[64,64,128]{2,1,0:T(8,128)(2,1)}, f32[2,128,64]{2,1,0:T(8,128)}, f32[16,8,128]{2,1,0:T(8,128)}) custom-call(bf16[64,64,128]{2,1,0:T(8,128)(2,1)} %inp.1, bf16[64,64,128]{2,1,0:T(8,128)(2,1)} %cot.1, bf16[2,8,8,4096]{3,2,1,0:T(8,128)(2,1)} %w.1, bf16[64,64]{1,0:T(8,128)(2,1)} %pw_hbm.1, f32[64]{0:T(128)} %bias_hbm.1, ...), custom_call_target="tpu_custom_call" | custom-call | tf_op jit(solution)/shard_map/pallas_call | solution.py:588
  123.6 2.9 %shard_map.103 = (bf16[64,64,128]{2,1,0:T(8,128)(2,1)}, f32[2,8,8,4096]{3,2,1,0:T(8,128)}, f32[64,64]{1,0:T(8,128)}, f32[1,64]{1,0:T(1,128)}) custom-call(bf16[64,64,128]{2,1,0:T(8,128)(2,1)} %get-tuple-element.11.gin, f32[2,128,64]{2,1,0:T(8,128)} %get-tuple-element.12.ug, f32[16,8,128]{2,1,0:T(8,128)} %get-tuple-element.13.zsum), custom_call_target="tpu_custom_call" | custom-call | tf_op jit(solution)/shard_map/pallas_call | solution.py:635

commit v6 on v5

--- a/solution.py
+++ b/solution.py
@@ -42,16 +42,11 @@
 @functools.cache
 def tables():
     cos, sin = trig(np.arange(K2), np.arange(NX), NX)
-    tx = np.stack([cos.reshape(N, 8, NX), -sin.reshape(N, 8, NX)], 1).reshape(2 * K2, 8, NX // 8)
-    tx = tx.transpose(1, 0, 2)
+    tx = np.concatenate([cos, -sin], 0).reshape(2 * K2, 8, NX // 8).transpose(1, 0, 2)
     cos, sin = trig(np.arange(K1) - K1 // 2, np.arange(NY), NY)
-    ty = np.stack([cos.reshape(K1, N, TY), sin.reshape(K1, N, TY)], 2).reshape(K1, 8, 256)
-    ty = ty.transpose(1, 0, 2).reshape(4, 256, 256)
     c4, s4 = (t.reshape(N, 8, N, TY).transpose(2, 3, 0, 1) for t in (cos, sin))
     back = np.stack([np.stack([c4, -s4], 3), np.stack([s4, c4], 3)], 1).reshape(N, 2 * TY, 2 * K1)
-    cos, sin = trig(np.arange(K2), np.arange(NX), NX)
-    txb = np.concatenate([cos, -sin], 0).reshape(2 * K2, 8, NX // 8).transpose(1, 0, 2)
-    return np.ascontiguousarray(np.concatenate([tx, ty, txb], 0)), np.ascontiguousarray(back)
+    return np.ascontiguousarray(tx), np.ascontiguousarray(back)
 
 
 def dot(a, b):
@@ -71,7 +66,7 @@
 def kernel(
     inp, cot, w, pw_hbm, bias_hbm, tab, back,
     gin, ug, zsum,
-    pw, bias, inp_v, cot_v, w_v, tab_v, back_v, e1_v, e_v, sel_v,
+    pw, bias, inp_v, cot_v, w_v, tab_v, back_v, backt_v, e1_v, e_v, sel_v,
     xr, yr, tr, xsend, ysend, tsend, gsend, gath,
     zsend, zr, f2_v, dz_v, dz2_v, kron_v, zp_v, gz_v, s_v, ug_v, gin_v,
     send_sem, recv_sem, loc_sem,
@@ -79,11 +74,6 @@
     row = lax.axis_index("row")
     col = lax.axis_index("col")
     col_x, col_y, col_c = lax.div(col, 8), lax.rem(lax.div(col, 2), 4), lax.rem(col, 2)
-    lane_lo = lax.broadcasted_iota(jnp.int32, (16, 128), 1) < 64
-    mask_j = (lax.broadcasted_iota(jnp.int32, (8, 8, 128), 2) & 7) == lax.broadcasted_iota(
-        jnp.int32, (8, 8, 128), 0
-    )
-
     mask_k = (lax.broadcasted_iota(jnp.int32, (8, 8, 128), 2) & 7) == lax.broadcasted_iota(
         jnp.int32, (8, 8, 128), 1
     )
@@ -151,33 +141,6 @@
             remote(src_of(m), dst.at[col], phase, 0, (row, m)).start()
         keep(src_of(col), dst.at[col], phase)
         sent(like, phase)
-
-    block = wrap(row + col)
-    top = row == 0
-
-    def send_t(src, dst, phase):
-        @pl.loop(0, N)
-        def _(i):
-            is_own = jnp.logical_and(top, i == row)
-
-            @pl.when(jnp.logical_not(is_own))
-            def _():
-                remote(src.at[i], dst.at[col], phase, 0, (i, block)).start()
-
-            @pl.when(is_own)
-            def _():
-                keep(src.at[i], dst.at[col], phase)
-
-        def wait():
-            @pl.when(top)
-            def _():
-                wait_sent(src.at[pl.ds(0, N - 1)], phase)
-
-            @pl.when(jnp.logical_not(top))
-            def _():
-                wait_sent(src, phase)
-
-        pending.append(wait)
 
     barrier = pltpu.get_barrier_semaphore()
 
@@ -240,7 +203,7 @@
                     dst[out, y : y + 16, :] = res[:, 128 * t : 128 * t + 128].reshape(16, 16, 128)
 
     def forward_x(src, phase, dst, half):
-        acc = jnp.zeros((256, 128), F32)
+        acc = jnp.zeros((128, 256), F32)
         for x, y in CHIPS:
             chip = 4 * (col_x ^ x) + lax.rem(col_y + y, 4)
             blocks = []
@@ -252,27 +215,19 @@
                     wait_recv(src.at[half, slot], phase, N * half + slot)
 
                 blocks.append(src[half, slot].reshape(128, 128))
-            acc = acc + dot_t(tab_v[chip], jnp.concatenate(blocks, 1))
-        dst[...] = acc.astype(BF).reshape(N, 16, 128)
+            acc = acc + dot_t(jnp.concatenate(blocks, 1), tab_v[chip])
+        acc = acc.astype(BF)
+        parts = [jnp.concatenate([acc[0:TY, at : at + 128], acc[TY : 2 * TY, at : at + 128]], 1) for at in (0, 128)]
+        dst[...] = dot(backt_v[...], jnp.concatenate(parts, 0)).astype(BF).reshape(N, 16, 256)
 
     def forward_y(src):
-        acc = jnp.zeros((K1, 32), F32)
-        for q in range(8):
-            parts = []
-            for t in range(2):
-                b = src[2 * q + t].astype(F32)
-                jb = jnp.concatenate([b[8:16], -b[0:8]], 0)
-                rows = [
-                    jnp.where(lane_lo, b, pltpu.roll(jb, 64, 1)),
-                    jnp.where(lane_lo, pltpu.roll(b, 64, 1), jb),
-                ]
-                parts.append(jnp.concatenate(rows, 0).astype(BF))
-            table = tab_v[8 + q // 2, 128 * (q % 2) : 128 * (q % 2) + 128, :]
-            acc = acc + dot_t(table, jnp.concatenate(parts, 1))
-        return (acc * SCALE).astype(BF).astype(F32).reshape(N, 8, 32)
-
-    def pack_t(first, second, dst):
-        dst[...] = jnp.concatenate([first[:, 0:4], second[:, 0:4], first[:, 4:8], second[:, 4:8]], 2)
+        total = jnp.sum(src[...].astype(F32), axis=0) * SCALE
+        return [total[:, 0:128], total[:, 128:256]]
+
+    def pack_t(tiles, dst):
+        xt = jnp.concatenate(tiles + [jnp.zeros((64, 128), F32)], 0).astype(BF).astype(F32)
+        x = xt.T.reshape(N, 8, 128)
+        dst[...] = jnp.concatenate([x[:, 0:4, 0:64], x[:, 4:8, 0:64]], 2)
 
     def unpack_t(src):
         x = src[...]
@@ -287,7 +242,7 @@
             for c in range(4):
                 at = (2 * c + ri) * 8
                 tile = xt[at : at + 8]
-                cols.append(jnp.where(mask_j, tile[None], 0.0).reshape(64, 128))
+                cols.append(jnp.where(mask_k, tile[:, None, :], 0.0).reshape(64, 128))
             rows.append(jnp.concatenate(cols, 1))
         return dot(jnp.concatenate(rows, 0).astype(BF), e1_v[...])
 
@@ -316,7 +271,7 @@
         late = None
         for x, y in CHIPS:
             chip = 4 * (col_x ^ x) + lax.rem(col_y + jnp.where(col_c == 0, y, 4 - y), 4)
-            res = (dot(yt, tab_v[12 + chip]) * SCALE).astype(BF)
+            res = (dot(yt, tab_v[chip]) * SCALE).astype(BF)
             for c in range(2):
                 out[half, 2 * chip + c] = res[:, 128 * c : 128 * c + 128].reshape(2, TY, TX)
             m = 2 * chip + col_c
@@ -349,13 +304,15 @@
         at = pl.ds(pl.multiple_of(i * 512, 512), 512)
         e_v[:, at] = jnp.where(channel == own, 1.0, 0.0).astype(BF)
 
+    loads[8].wait()
+    backt_v[...] = back_v[...].astype(F32).T.astype(BF)
     loads[3].wait()
     loads[4].wait()
     loads[5].wait()
     for half in range(2):
         forward_x(xr.at[0], X1, ysend.at[0, half], half)
         send_row(
-            lambda r, half=half: ysend.at[0, half, wrap(r + col)],
+            lambda r, half=half: ysend.at[0, half, r],
             yr.at[0, half],
             Y1,
             row,
@@ -366,10 +323,9 @@
     wait_recv(yr.at[0, 0], Y1, 0)
     first_half = forward_y(yr.at[0, 0])
     wait_recv(yr.at[0, 1], Y1, 1)
-    pack_t(first_half, forward_y(yr.at[0, 1]), tsend.at[0])
-    send_t(tsend.at[0], tr.at[0], T1)
+    pack_t(first_half + forward_y(yr.at[0, 1]), tsend.at[0])
+    send_col(lambda m: tsend.at[0, m], tr.at[0], T1, tsend.at[0, pl.ds(0, N - 1)])
     loads[6].wait()
-    loads[8].wait()
     wait_recv(tr.at[0], T1)
 
     u = to_modes(tr.at[0])
@@ -459,20 +415,20 @@
     apply_kron(1, dz2_v, gz_v)
 
     for half in range(2):
-        forward_x(xr.at[2], X3, ysend.at[2, half], half)
+        forward_x(xr.at[2], X3, ysend.at[1, half], half)
         send_row(
-            lambda r, half=half: ysend.at[2, half, wrap(r + col)],
-            yr.at[2, half],
+            lambda r, half=half: ysend.at[1, half, r],
+            yr.at[1, half],
             Y3,
             row,
-            ysend.at[2, half, pl.ds(0, N - 1)],
+            ysend.at[1, half, pl.ds(0, N - 1)],
             half,
         )
-    wait_recv(yr.at[2, 0], Y3, 0)
-    first_half = forward_y(yr.at[2, 0])
-    wait_recv(yr.at[2, 1], Y3, 1)
-    pack_t(first_half, forward_y(yr.at[2, 1]), tsend.at[2])
-    send_t(tsend.at[2], tr.at[2], T3)
+    wait_recv(yr.at[1, 0], Y3, 0)
+    first_half = forward_y(yr.at[1, 0])
+    wait_recv(yr.at[1, 1], Y3, 1)
+    pack_t(first_half + forward_y(yr.at[1, 1]), tsend.at[2])
+    send_col(lambda m: tsend.at[2, m], tr.at[2], T3, tsend.at[2, pl.ds(0, N - 1)])
     wait_recv(zr.at[0], Z1)
     zr[3, 0] = jnp.sum(zr[0], axis=0)
     send_row(lambda r: zr.at[3, 0], zr.at[1], Z2, row, zsend.at[pl.ds(0, N - 1)])
@@ -602,14 +558,15 @@
             pltpu.VMEM((2, 8, 8, C * C), BF),
             pltpu.VMEM(table.shape, BF),
             pltpu.VMEM(back.shape[1:], BF),
+            pltpu.VMEM((256, 128), BF),
             pltpu.VMEM((512, 64), BF),
             pltpu.VMEM((64, C * C), BF),
             pltpu.VMEM((1024, 64), BF),
             pltpu.VMEM((4, 2, N, 2, TY, TX), BF),
-            pltpu.VMEM((4, 2, N, 16, 128), BF),
+            pltpu.VMEM((2, 2, N, 16, 256), BF),
             pltpu.VMEM((4, N, 4, 128), F32),
             pltpu.VMEM((2, 2, N, 2, TY, TX), BF),
-            pltpu.VMEM((4, 2, N, 16, 128), BF),
+            pltpu.VMEM((2, 2, N, 16, 256), BF),
             pltpu.VMEM((4, N, 4, 128), F32),
             pltpu.VMEM((2, 2, 16, 256), BF),
             pltpu.VMEM((2, 2, N, 16, 256), BF),

time: 127 us -> 120 us (0.945)
  Pallas kernels: 126 us -> 120 us
    pallas_call x1, Pallas kernels: 123 us -> 117 us  [body(): pl.pallas_call(kernel, out_shape=(jax.ShapeDtypeStruct(field, BF), jax.Sh...]
where the time goes in v6:
time: 120 us
  Pallas kernels  120 us (100%)
    pallas_call x1, Pallas kernels, body(): pl.pallas_call(kernel, out_shape=(jax.ShapeDtypeStruct(field, BF), jax.Sh...  117 us
    pallas_call x1, Pallas kernels, body(): pl.pallas_call(last_kernel, out_shape=(jax.ShapeDtypeStruct(field, BF), j...  2.91 us

profile of v6, /device:TPU:1, one launch (start us, length us, event | category | flops | bytes accessed | tf_op | source)
XLA Modules:
  0.0 120.3 jit_solution(6155827484156260106)
XLA Ops:
  0.6 116.7 %shard_map.102 = (bf16[64,64,128]{2,1,0:T(8,128)(2,1)}, f32[2,128,64]{2,1,0:T(8,128)}, f32[16,8,128]{2,1,0:T(8,128)}) custom-call(bf16[64,64,128]{2,1,0:T(8,128)(2,1)} %inp.1, bf16[64,64,128]{2,1,0:T(8,128)(2,1)} %cot.1, bf16[2,8,8,4096]{3,2,1,0:T(8,128)(2,1)} %w.1, bf16[64,64]{1,0:T(8,128)(2,1)} %pw_hbm.1, f32[64]{0:T(128)} %bias_hbm.1, ...), custom_call_target="tpu_custom_call" | custom-call | tf_op jit(solution)/shard_map/pallas_call | solution.py:544
  117.3 2.9 %shard_map.103 = (bf16[64,64,128]{2,1,0:T(8,128)(2,1)}, f32[2,8,8,4096]{3,2,1,0:T(8,128)}, f32[64,64]{1,0:T(8,128)}, f32[1,64]{1,0:T(1,128)}) custom-call(bf16[64,64,128]{2,1,0:T(8,128)(2,1)} %get-tuple-element.11.gin, f32[2,128,64]{2,1,0:T(8,128)} %get-tuple-element.12.ug, f32[16,8,128]{2,1,0:T(8,128)} %get-tuple-element.13.zsum), custom_call_target="tpu_custom_call" | custom-call | tf_op jit(solution)/shard_map/pallas_call | solution.py:592

commit v7 on v6

--- a/solution.py
+++ b/solution.py
@@ -66,7 +66,7 @@
 def kernel(
     inp, cot, w, pw_hbm, bias_hbm, tab, back,
     gin, ug, zsum,
-    pw, bias, inp_v, cot_v, w_v, tab_v, back_v, backt_v, e1_v, e_v, sel_v,
+    pw, bias, inp_v, cot_v, w_v, wide_v, tab_v, back_v, backt_v, e1_v, e_v, sel_v,
     xr, yr, tr, xsend, ysend, tsend, gsend, gath,
     zsend, zr, f2_v, dz_v, dz2_v, kron_v, zp_v, gz_v, s_v, ug_v, gin_v,
     send_sem, recv_sem, loc_sem,
@@ -144,10 +144,11 @@
 
     barrier = pltpu.get_barrier_semaphore()
 
-    @pl.loop(1, N)
-    def _(d):
-        pl.semaphore_signal(barrier, inc=1, device_id=(row, wrap(col + d)), device_id_type=MESH)
-        pl.semaphore_signal(barrier, inc=1, device_id=(wrap(row + d), col), device_id_type=MESH)
+    for x, z in ROW_ORDER:
+        pl.semaphore_signal(barrier, inc=1, device_id=(row_partner(x, z), col), device_id_type=MESH)
+    for x, y, c in COL_ORDER:
+        m = col_partner(x, y, c, col_c)
+        pl.semaphore_signal(barrier, inc=1, device_id=(row, m), device_id_type=MESH)
 
     loads = [
         pltpu.make_async_copy(src, dst, loc_sem.at[i])
@@ -326,6 +327,13 @@
     pack_t(first_half + forward_y(yr.at[0, 1]), tsend.at[0])
     send_col(lambda m: tsend.at[0, m], tr.at[0], T1, tsend.at[0, pl.ds(0, N - 1)])
     loads[6].wait()
+
+    @pl.loop(0, 8)
+    def _(i):
+        at = pl.ds(pl.multiple_of(i * 512, 512), 512)
+        for p in range(2):
+            wide_v[p, :, at] = w_v[p, :, :, at].astype(F32).reshape(64, 512)
+
     wait_recv(tr.at[0], T1)
 
     u = to_modes(tr.at[0])
@@ -340,8 +348,7 @@
         at = pl.ds(pl.multiple_of(i * 512, 512), 512)
         ue = dot(u, e_v[:, at])
         ur, ui = ue[0:64], ue[64:128]
-        wr = w_v[0, :, :, at].astype(F32).reshape(64, 512)
-        wi = w_v[1, :, :, at].astype(F32).reshape(64, 512)
+        wr, wi = wide_v[0, :, at], wide_v[1, :, at]
         return sr + fold(wr * ur - wi * ui), si + fold(wr * ui + wi * ur)
 
     zero = jnp.zeros((64, 128), F32)
@@ -442,8 +449,7 @@
 
     def mix_back(i, acc):
         at = pl.ds(pl.multiple_of(i * 512, 512), 512)
-        wr = w_v[0, :, :, at].astype(F32).reshape(64, 512)
-        wi = w_v[1, :, :, at].astype(F32).reshape(64, 512)
+        wr, wi = wide_v[0, :, at], wide_v[1, :, at]
         both = jnp.concatenate([wr * gr4 + wi * gi4, wr * gi4 - wi * gr4], 0).astype(BF)
         return acc + dot_t(both, e_v[:, at])
 
@@ -451,9 +457,6 @@
     from_modes(du, tsend.at[3])
     send_col(lambda m: tsend.at[3, m], tr.at[3], T4, tsend.at[3, pl.ds(0, N - 1)])
 
-    wait_recv(zr.at[1], Z2)
-    zr[3, 1] = jnp.sum(zr[1], axis=0)
-    send_col(lambda m: zr.at[3, 1], zr.at[2], Z3, zsend.at[pl.ds(0, N - 1)])
     out_ug = pltpu.make_async_copy(ug_v, ug, loc_sem.at[0])
     out_ug.start()
     pending.append(out_ug.wait)
@@ -469,13 +472,16 @@
             gath.at[1, half, pl.ds(0, N - 1)],
             half,
         )
+    wait_recv(zr.at[1], Z2)
+    zr[3, 1] = jnp.sum(zr[1], axis=0)
+    send_col(lambda m: zr.at[3, 1], zr.at[2], Z3, zsend.at[pl.ds(0, N - 1)])
+    for half in range(2):
+        wait_recv(gath.at[1, half], Y4, half)
+        inverse_x(gath.at[1, half], xsend.at[1], xr.at[3], X4, half)
     wait_recv(zr.at[2], Z3)
     out_z = pltpu.make_async_copy(zr.at[2], zsum, loc_sem.at[2])
     out_z.start()
     pending.append(out_z.wait)
-    for half in range(2):
-        wait_recv(gath.at[1, half], Y4, half)
-        inverse_x(gath.at[1, half], xsend.at[1], xr.at[3], X4, half)
     finish()
 
     def finish_block(m, half):
@@ -556,6 +562,7 @@
             pltpu.VMEM(field, BF),
             pltpu.VMEM(field, BF),
             pltpu.VMEM((2, 8, 8, C * C), BF),
+            pltpu.VMEM((2, 64, C * C), F32),
             pltpu.VMEM(table.shape, BF),
             pltpu.VMEM(back.shape[1:], BF),
             pltpu.VMEM((256, 128), BF),

time: 120 us -> 120 us (level)
  no operation moved by 1% of the time
where the time goes in v7:
time: 120 us
  Pallas kernels  120 us (100%)
    pallas_call x1, Pallas kernels, body(): pl.pallas_call(kernel, out_shape=(jax.ShapeDtypeStruct(field, BF), jax.Sh...  117 us
    pallas_call x1, Pallas kernels, body(): pl.pallas_call(last_kernel, out_shape=(jax.ShapeDtypeStruct(field, BF), j...  2.91 us

profile of v7, /device:TPU:1, one launch (start us, length us, event | category | flops | bytes accessed | tf_op | source)
XLA Modules:
  0.0 120.1 jit_solution(1056038871860426097)
XLA Ops:
  0.6 116.6 %shard_map.102 = (bf16[64,64,128]{2,1,0:T(8,128)(2,1)}, f32[2,128,64]{2,1,0:T(8,128)}, f32[16,8,128]{2,1,0:T(8,128)}) custom-call(bf16[64,64,128]{2,1,0:T(8,128)(2,1)} %inp.1, bf16[64,64,128]{2,1,0:T(8,128)(2,1)} %cot.1, bf16[2,8,8,4096]{3,2,1,0:T(8,128)(2,1)} %w.1, bf16[64,64]{1,0:T(8,128)(2,1)} %pw_hbm.1, f32[64]{0:T(128)} %bias_hbm.1, ...), custom_call_target="tpu_custom_call" | custom-call | tf_op jit(solution)/shard_map/pallas_call | solution.py:550
  117.2 2.9 %shard_map.103 = (bf16[64,64,128]{2,1,0:T(8,128)(2,1)}, f32[2,8,8,4096]{3,2,1,0:T(8,128)}, f32[64,64]{1,0:T(8,128)}, f32[1,64]{1,0:T(1,128)}) custom-call(bf16[64,64,128]{2,1,0:T(8,128)(2,1)} %get-tuple-element.11.gin, f32[2,128,64]{2,1,0:T(8,128)} %get-tuple-element.12.ug, f32[16,8,128]{2,1,0:T(8,128)} %get-tuple-element.13.zsum), custom_call_target="tpu_custom_call" | custom-call | tf_op jit(solution)/shard_map/pallas_call | solution.py:599
